TPU v7x, 128 devices: a whole 4x4x4 slice. The times are simulated.
128 devices in a mesh: gx: 8 (over x_lo, z), gy: 16 (over y, x_hi, core).
Axes of the slice: x: 4 (x_hi: 2, x_lo: 2; x = x_hi * 2 + x_lo), y: 4, z: 4, core: 2. Of those that a mesh axis runs over, the one named last changes fastest.
Arguments:
- ice_force: float32 [2, 11, 256, 2048], P(None, None, 'gx', 'gy'), may hold values from -6 to 6
- ice_visc: float32 [10, 256, 2048], P(None, 'gx', 'gy'), may hold values from 0.2 to 5
- ice_drag: float32 [256, 2048], P('gx', 'gy'), may hold values from 0.5 to 5
- ice_mask: int32 [256, 2048], P('gx', 'gy'), may hold values 0 or 1
- ice_thick: float32 [256, 2048], P('gx', 'gy'), may hold values from 0.1 to 1.5
- ice_target: int32 [4096], P(('gx', 'gy')), may hold values from -1 to 4095, as said below
- ocean_temp: float32 [80, 256, 2048], P(None, 'gx', 'gy'), may hold values from -2 to 1
- ocean_salt: float32 [80, 256, 2048], P(None, 'gx', 'gy'), may hold values from -2 to 2
- ocean_diff: float32 [256, 2048], P('gx', 'gy'), may hold values from 0.05 to 0.2
- ocean_mask: int32 [256, 2048], P('gx', 'gy'), may hold values 0 or 1
- ocean_source: int32 [4096], P(('gx', 'gy')), may hold values from 0 to 4095, as said below
Outputs:
- ice_velocity: float32 [2, 11, 256, 2048], P(None, None, 'gx', 'gy')
- ice_thick_new: float32 [256, 2048], P('gx', 'gy')
- ocean_temp_new: float32 [80, 256, 2048], P(None, 'gx', 'gy')
- ocean_salt_new: float32 [80, 256, 2048], P(None, 'gx', 'gy')
Inputs may be any that keep to these rules, and one draw needn't show every extreme that they name: ice_target and ocean_source are inverse lists: every ocean block has exactly one ice block above it, no ice block feeds two; each ocean device takes exactly 1 block from each of its 32 source devices, so at most 1 block pass between any two devices and that bound is reached. `ice_target`: -1 for ice blocks over no cavity; each device has exactly 32 coupled blocks.
All inputs are finite; a program needn't handle non-finite values. No bound on the sum of `ice_mask` or of `ocean_mask` on one device may be relied on, other than what follows from the above.
Results may differ from a plain program's by a relative error of at most 0.0001.
Values sent between devices are 32-bit elements; how exact they have to be, the bound alone decides.
A program may use at most 128 MiB of HBM per device.

v0:
```python
import jax
import jax.numpy as jnp
import numpy as np
from jax import lax
from jax.sharding import PartitionSpec as P

SUBSTEPS = 4
MATVECS = 3


relax_weight = 0.6
shift_term = 0.2
vert_mix = 0.1
heat_gamma = 0.5
heat_factor = 0.05
salt_factor = 0.05
salt_ref = 34.5
freeze_slope = -0.0573
freeze_base = 0.0832
freeze_depth = 0.761
melt_factor = 0.2
draft_ratio = 0.89


def extended(cells, sides, width):
    for axis, dim in sides:
        count = lax.axis_size(axis)
        ends = count - 1
        head = lax.slice_in_dim(cells, 0, width, axis=dim)
        tail = lax.slice_in_dim(cells, cells.shape[dim] - width, cells.shape[dim], axis=dim)
        cells = jnp.concatenate(
            [
                lax.ppermute(tail, axis, [(i, (i + 1) % count) for i in range(ends)]),
                cells,
                lax.ppermute(head, axis, [((i + 1) % count, i) for i in range(ends)]),
            ],
            axis=dim,
        )
    return cells


def from_behind(shard, axis, by):
    size = lax.axis_size(axis)
    pairs = [(i, i + by) for i in range(size) if 0 <= i + by < size]
    return lax.ppermute(shard, axis, pairs)


def element_table():
    gauss = [0.5 - 0.5 / np.sqrt(3.0), 0.5 + 0.5 / np.sqrt(3.0)]
    element_matrix = np.zeros((16, 16))
    for point_z in gauss:
        for point_x in gauss:
            for point_y in gauss:
                gradients = np.zeros((8, 3))
                for corner in range(8):
                    depth_off = corner // 4
                    row_off = corner // 2 % 2
                    col_off = corner % 2
                    shape_z = point_z if depth_off else 1.0 - point_z
                    shape_x = point_x if row_off else 1.0 - point_x
                    shape_y = point_y if col_off else 1.0 - point_y
                    sign_z = 1.0 if depth_off else -1.0
                    sign_x = 1.0 if row_off else -1.0
                    sign_y = 1.0 if col_off else -1.0
                    gradients[corner] = [
                        sign_x * shape_y * shape_z,
                        sign_y * shape_x * shape_z,
                        sign_z * shape_x * shape_y,
                    ]
                for first in range(8):
                    for second in range(8):
                        grad_a = gradients[first]
                        grad_b = gradients[second]
                        element_matrix[first, second] += 0.125 * (
                            4 * grad_a[0] * grad_b[0]
                            + grad_a[1] * grad_b[1]
                            + grad_a[2] * grad_b[2]
                        )
                        element_matrix[first, 8 + second] += 0.125 * (
                            2 * grad_a[0] * grad_b[1] + grad_a[1] * grad_b[0]
                        )
                        element_matrix[8 + first, second] += 0.125 * (
                            2 * grad_a[1] * grad_b[0] + grad_a[0] * grad_b[1]
                        )
                        element_matrix[8 + first, 8 + second] += 0.125 * (
                            4 * grad_a[1] * grad_b[1]
                            + grad_a[0] * grad_b[0]
                            + grad_a[2] * grad_b[2]
                        )
    return element_matrix.astype(np.float32)


def corner_stack(nodes):
    layer_count = nodes.shape[1] - 1
    row_count = nodes.shape[2] - 2
    col_count = nodes.shape[3] - 2
    portions = []
    for component in range(2):
        for corner in range(8):
            depth_off = corner // 4
            row_off = corner // 2 % 2
            col_off = corner % 2
            portions.append(
                nodes[
                    component,
                    depth_off : depth_off + layer_count,
                    row_off : row_off + row_count + 1,
                    col_off : col_off + col_count + 1,
                ]
            )
    return jnp.stack(portions)


def scatter_owned(values, row_count, col_count):
    components = []
    zero_level = jnp.zeros((1, row_count, col_count), jnp.float32)
    for component in range(2):
        summed = None
        for corner in range(8):
            depth_off = corner // 4
            row_off = corner // 2 % 2
            col_off = corner % 2
            portion = values[
                component * 8 + corner,
                :,
                1 - row_off : 1 - row_off + row_count,
                1 - col_off : 1 - col_off + col_count,
            ]
            if depth_off:
                portion = jnp.concatenate([zero_level, portion], 0)
            else:
                portion = jnp.concatenate([portion, zero_level], 0)
            summed = portion if summed is None else summed + portion
        components.append(summed)
    return jnp.stack(components)


def apply_operator(nodes, weights_ext, element_matrix):
    row_count = nodes.shape[2] - 2
    col_count = nodes.shape[3] - 2
    stacked = corner_stack(nodes)
    products = jnp.einsum("ab,bkij->akij", element_matrix, stacked, precision=lax.Precision.HIGHEST)
    products = products * weights_ext[None, :, : row_count + 1, : col_count + 1]
    return scatter_owned(products, row_count, col_count)


def ice_solve(force, weights_ext, drag, element_matrix, extend):
    levels = force.shape[1]
    row_count = force.shape[2]
    col_count = force.shape[3]
    diag_extra = shift_term + jnp.concatenate(
        [drag[None], jnp.zeros((levels - 1, row_count, col_count), jnp.float32)], 0
    )
    diag_values = (
        jnp.diagonal(element_matrix)[:, None, None, None]
        * weights_ext[None, :, : row_count + 1, : col_count + 1]
    )
    diagonal = scatter_owned(diag_values, row_count, col_count) + diag_extra[None]
    velocity = relax_weight * force / diagonal
    for iteration in range(MATVECS):
        applied = (
            apply_operator(extend(velocity), weights_ext, element_matrix)
            + diag_extra[None] * velocity
        )
        velocity = velocity + relax_weight * (force - applied) / diagonal
    return velocity


def freezing(salt_top, draft):
    return freeze_slope * (salt_ref + salt_top) + freeze_base - freeze_depth * draft


def ocean_substep(fields, static):
    row_count = fields.shape[2] - 2
    col_count = fields.shape[3] - 2
    center = fields[:, :, 1:-1, 1:-1]
    diff_mid = static[0, 1:-1, 1:-1]
    wet_mid = static[1, 1:-1, 1:-1]
    draft_mid = static[2, 1:-1, 1:-1]
    lateral = jnp.zeros_like(center)
    for row_start, col_start in ((0, 1), (2, 1), (1, 0), (1, 2)):
        diff_near = static[0, row_start : row_start + row_count, col_start : col_start + col_count]
        wet_near = static[1, row_start : row_start + row_count, col_start : col_start + col_count]
        near = fields[:, :, row_start : row_start + row_count, col_start : col_start + col_count]
        lateral = lateral + 0.5 * (diff_mid + diff_near) * wet_mid * wet_near * (near - center)
    vert_flux = vert_mix * (center[:, 1:] - center[:, :-1])
    zero_level = jnp.zeros((2, 1, row_count, col_count), jnp.float32)
    vertical = jnp.concatenate([vert_flux, zero_level], 1) - jnp.concatenate(
        [zero_level, vert_flux], 1
    )
    updated = center + lateral + wet_mid * vertical
    temp_top = updated[0, 0]
    salt_top = updated[1, 0]
    melt_rate = heat_gamma * (temp_top - freezing(salt_top, draft_mid)) * wet_mid
    updated = updated.at[0, 0].set(temp_top - heat_factor * melt_rate)
    updated = updated.at[1, 0].set(
        salt_top - salt_factor * melt_rate * (salt_ref + salt_top) / salt_ref
    )
    return updated


def sender_table(targets, ocean_rows, slot_total, capacity):
    coupled = targets >= 0
    target_dev = jnp.where(coupled, targets // ocean_rows, 0)
    positions = jnp.arange(targets.shape[0], dtype=jnp.int32)
    earlier = (
        (target_dev[:, None] == target_dev[None, :])
        & coupled[None, :]
        & (positions[None, :] < positions[:, None])
    )
    slot_rank = jnp.sum(earlier.astype(jnp.int32), axis=1)
    keyed = target_dev * capacity + slot_rank
    slots = jnp.arange(slot_total, dtype=jnp.int32)
    return ((keyed[None, :] == slots[:, None]) & coupled[None, :]).astype(jnp.float32)


def receiver_table(sources, ice_rows, slot_total, capacity):
    source_dev = sources // ice_rows
    source_row = sources % ice_rows
    earlier = (source_dev[:, None] == source_dev[None, :]) & (
        source_row[None, :] < source_row[:, None]
    )
    slot_rank = jnp.sum(earlier.astype(jnp.int32), axis=1)
    keyed = source_dev * capacity + slot_rank
    slots = jnp.arange(slot_total, dtype=jnp.int32)
    return (keyed[:, None] == slots[None, :]).astype(jnp.float32)


def extend_nodes(velocity):
    return extended(velocity, (("gx", 2), ("gy", 3)), 1)


def per_device(
    ice_force,
    ice_visc,
    ice_drag,
    ice_mask,
    ice_thick,
    ice_target,
    ocean_temp,
    ocean_salt,
    ocean_diff,
    ocean_mask,
    ocean_source,
):
    element_matrix = jnp.asarray(element_table())
    ice_rows = ice_thick.shape[0]
    col_count = ice_thick.shape[1]
    ocean_rows = ocean_diff.shape[0]
    size_x = lax.axis_size("gx")
    size_y = lax.axis_size("gy")
    capacity = max(1, 2 * ocean_rows // (size_x * size_y))
    slot_total = size_x * size_y * capacity
    ice_wet = ice_mask.astype(jnp.float32)
    send_map = sender_table(ice_target, ocean_rows, slot_total, capacity)
    recv_map = receiver_table(ocean_source, ice_rows, slot_total, capacity)
    outgoing = jnp.dot(send_map, draft_ratio * ice_thick, precision=lax.Precision.HIGHEST)
    incoming = lax.all_to_all(
        outgoing.reshape(size_x * size_y, capacity, col_count),
        ("gx", "gy"),
        split_axis=0,
        concat_axis=0,
        tiled=True,
    ).reshape(slot_total, col_count)
    ocean_draft = jnp.dot(recv_map, incoming, precision=lax.Precision.HIGHEST)
    weights = ice_visc * ice_wet[None]
    row_before = from_behind(weights[:, -1:, :], "gx", 1)
    with_row = jnp.concatenate([row_before, weights], 1)
    column_before = from_behind(with_row[:, :, -1:], "gy", 1)
    weights_ext = jnp.concatenate([column_before, with_row], 2)
    velocity = ice_solve(ice_force, weights_ext, ice_drag, element_matrix, extend_nodes)
    wet = ocean_mask.astype(jnp.float32)
    static = jnp.stack([ocean_diff, wet, ocean_draft])
    fields = jnp.stack([ocean_temp, ocean_salt])
    static_ext = extended(static, (("gx", 1), ("gy", 2)), 1)
    for substep_index in range(SUBSTEPS):
        widened = extended(fields, (("gx", 2), ("gy", 3)), 1)
        fields = ocean_substep(widened, static_ext)
    melt_rate = heat_gamma * (fields[0, 0] - freezing(fields[1, 0], ocean_draft)) * wet
    returning = jnp.dot(recv_map.T, melt_rate, precision=lax.Precision.HIGHEST)
    arrived = lax.all_to_all(
        returning.reshape(size_x * size_y, capacity, col_count),
        ("gx", "gy"),
        split_axis=0,
        concat_axis=0,
        tiled=True,
    ).reshape(slot_total, col_count)
    ice_melt = jnp.dot(send_map.T, arrived, precision=lax.Precision.HIGHEST)
    ice_thick_new = ice_thick - melt_factor * ice_melt * ice_wet
    return (velocity, ice_thick_new, fields[0], fields[1])


def solution(mesh):
    in_specs = (
        P(None, None, "gx", "gy"),
        P(None, "gx", "gy"),
        P("gx", "gy"),
        P("gx", "gy"),
        P("gx", "gy"),
        P(("gx", "gy")),
        P(None, "gx", "gy"),
        P(None, "gx", "gy"),
        P("gx", "gy"),
        P("gx", "gy"),
        P(("gx", "gy")),
    )
    out_specs = (P(None, None, "gx", "gy"), P("gx", "gy"), P(None, "gx", "gy"), P(None, "gx", "gy"))
    return jax.shard_map(
        per_device, mesh=mesh, in_specs=in_specs, out_specs=out_specs, check_vma=False
    )
```

profile of v0, /device:TPU:0, one launch (start us, length us, event | category | flops | bytes accessed | tf_op | source)
XLA Modules:
  0.0 368.4 jit_solution(9139900925356968098)
XLA Ops:
  2.4 3.9 %collective-permute-start = (f32[10,1,128]{2,1,0:T(1,128)S(1)}, f32[10,1,128]{2,1,0:T(1,128)S(1)}, u32[]{:S(2)}, u32[]{:S(2)}) collective-permute-start(f32[10,1,128]{2,1,0:T(1,128)S(1)} %slice.1076), channel_id=1, source_target_pairs={{0,16},{16,32},{32,48},{48,64},{64,80},{80,96},{96,112},{1,17},{17... | collective-permute-start | bytes 15368 | tf_op jit(solution)/shard_map/ppermute | solution.py:45
  6.3 2.1 fusion.82
  9.6 5.2 %collective-permute-start.15 = (f32[2,80,1,128]{3,2,1,0:T(1,128)}, f32[2,80,1,128]{3,2,1,0:T(1,128)}, u32[]{:S(2)}, u32[]{:S(2)}) collective-permute-start(f32[2,80,1,128]{3,2,1,0:T(1,128)} %get-tuple-element.196), channel_id=1, source_target_pairs={{0,16},{16,32},{32,48},{48,64},{64,80},{80,96},{96,112},{1,17},{17... | collective-permute-start | bytes 245768 | tf_op jit(solution)/shard_map/ppermute | solution.py:33
  15.5 1.3 collective-permute-start.1
  21.7 4.5 %collective-permute-start.2 = (f32[2,11,1,128]{3,2,1,0:T(1,128)S(1)}, f32[2,11,1,128]{3,2,1,0:T(1,128)S(1)}, u32[]{:S(2)}, u32[]{:S(2)}) collective-permute-start(f32[2,11,1,128]{3,2,1,0:T(1,128)S(1)} %get-tuple-element.214), channel_id=1, source_target_pairs={{0,16},{16,32},{32,48},{48,64},{64,80},{80,96},{96,112},{1,17},{17... | collective-permute-start | bytes 33800 | tf_op jit(solution)/shard_map/ppermute | solution.py:33
  26.3 1.3 collective-permute-done.2
  29.1 7.3 %collective-permute-start.4 = (f32[2,11,34,1]{3,2,1,0:T(8,128)S(1)}, f32[2,11,34,1]{3,2,1,0:T(8,128)S(1)}, u32[]{:S(2)}, u32[]{:S(2)}) collective-permute-start(f32[2,11,34,1]{3,2,1,0:T(8,128)S(1)} %get-tuple-element.203), channel_id=1, source_target_pairs={{0,1},{1,2},{2,3},{3,4},{4,5},{5,6},{6,7},{7,8},{8,9},{9,10},{10,1... | collective-permute-start | bytes 8984 | tf_op jit(solution)/shard_map/ppermute | solution.py:33
  38.9 8.4 %fusion.7 = f32[10,33,129,16]{2,3,1,0:T(8,128)S(1)} fusion(f32[16,16,1,1]{1,0,3,2:T(8,128)S(1)} %copy-done.52, f32[16,10,33,129]{3,2,1,0:T(8,128)S(1)} %slice_dynamic-update-slice_fusion.32), kind=kOutput, calls=%fused_computation.11 | convolution fusion | flops 130775040 | bytes 5449984 | tf_op jit(solution)/shard_map/ab,bkij->akij/dot_general | solution.py:142
  47.3 3.4 fusion.2
  53.0 4.5 %collective-permute-start.6 = (f32[2,11,1,128]{3,2,1,0:T(1,128)S(1)}, f32[2,11,1,128]{3,2,1,0:T(1,128)S(1)}, u32[]{:S(2)}, u32[]{:S(2)}) collective-permute-start(f32[2,11,1,128]{3,2,1,0:T(1,128)S(1)} %get-tuple-element.212), channel_id=1, source_target_pairs={{0,16},{16,32},{32,48},{48,64},{64,80},{80,96},{96,112},{1,17},{17... | collective-permute-start | bytes 33800 | tf_op jit(solution)/shard_map/ppermute | solution.py:33
  58.4 27.6 %all-to-all-start = ((f32[128,1,128]{2,1,0:T(1,128)}), f32[128,1,128]{2,1,0:T(1,128)}, u32[]{:S(2)}, u32[]{:S(2)}) async-start(f32[128,1,128]{2,1,0:T(1,128)} %bitcast.85), calls=%async_computation | async-start | bytes 131072 | tf_op jit(solution)/shard_map/all_to_all | solution.py:258
  86.3 1.3 collective-permute-start.9
  87.6 3.1 collective-permute-start.8
  90.7 1.4 collective-permute-done.8
  93.1 8.4 %fusion.5 = f32[10,33,129,16]{2,3,1,0:T(8,128)S(1)} fusion(f32[16,16,1,1]{1,0,3,2:T(8,128)S(1)} %copy-done.52, f32[16,10,33,129]{3,2,1,0:T(8,128)S(1)} %slice_dynamic-update-slice_fusion.16), kind=kOutput, calls=%fused_computation.9 | convolution fusion | flops 130775040 | bytes 5449984 | tf_op jit(solution)/shard_map/ab,bkij->akij/dot_general | solution.py:142
  101.6 3.6 fusion.1
  108.7 4.5 %collective-permute-start.10 = (f32[2,11,1,128]{3,2,1,0:T(1,128)S(1)}, f32[2,11,1,128]{3,2,1,0:T(1,128)S(1)}, u32[]{:S(2)}, u32[]{:S(2)}) collective-permute-start(f32[2,11,1,128]{3,2,1,0:T(1,128)S(1)} %get-tuple-element.210), channel_id=1, source_target_pairs={{0,16},{16,32},{32,48},{48,64},{64,80},{80,96},{96,112},{1,17},{17... | collective-permute-start | bytes 33800 | tf_op jit(solution)/shard_map/ppermute | solution.py:33
  113.3 1.9 fusion.63
  116.8 8.1 %collective-permute-start.12 = (f32[2,11,34,1]{3,2,1,0:T(8,128)S(1)}, f32[2,11,34,1]{3,2,1,0:T(8,128)S(1)}, u32[]{:S(2)}, u32[]{:S(2)}) collective-permute-start(f32[2,11,34,1]{3,2,1,0:T(8,128)S(1)} %get-tuple-element.199), channel_id=1, source_target_pairs={{0,1},{1,2},{2,3},{3,4},{4,5},{5,6},{6,7},{7,8},{8,9},{9,10},{10,1... | collective-permute-start | bytes 8984 | tf_op jit(solution)/shard_map/ppermute | solution.py:33
  127.3 8.4 %fusion.3 = f32[10,33,129,16]{2,3,1,0:T(8,128)S(1)} fusion(f32[16,16,1,1]{1,0,3,2:T(8,128)S(1)} %copy-done.52, f32[16,10,33,129]{3,2,1,0:T(8,128)S(1)} %slice_dynamic-update-slice_fusion), kind=kOutput, calls=%fused_computation.7 | convolution fusion | flops 130775040 | bytes 5449984 | tf_op jit(solution)/shard_map/ab,bkij->akij/dot_general | solution.py:142
  135.7 6.1 %fusion = f32[16,10,33,129]{3,2,1,0:T(8,128)} fusion(f32[10,33,129,16]{2,3,1,0:T(8,128)S(1)} %fusion.3, f32[10,33,129]{2,1,0:T(8,128)S(1)} %maximum_maximum_fusion.3), kind=kLoop, calls=%fused_computation.2 | loop fusion | flops 681120 | bytes 5619240 | tf_op jit(solution)/shard_map/mul | solution.py:143
  144.2 4.5 %collective-permute-start.14 = (f32[3,1,128]{2,1,0:T(1,128)S(1)}, f32[3,1,128]{2,1,0:T(1,128)S(1)}, u32[]{:S(2)}, u32[]{:S(2)}) collective-permute-start(f32[3,1,128]{2,1,0:T(1,128)S(1)} %get-tuple-element.220), channel_id=1, source_target_pairs={{0,16},{16,32},{32,48},{48,64},{64,80},{80,96},{96,112},{1,17},{17... | collective-permute-start | bytes 4616 | tf_op jit(solution)/shard_map/ppermute | solution.py:33
  148.7 4.2 %slice_bitcast_fusion.17 = (f32[10,32,128]{2,1,0:T(8,128)S(1)}, f32[10,32,128]{2,1,0:T(8,128)}, f32[10,32,128]{2,1,0:T(8,128)}, f32[10,32,128]{2,1,0:T(8,128)}, ...) fusion(f32[16,10,33,129]{3,2,1,0:T(8,128)} %fusion), kind=kLoop, calls=%fused_computation.230 | loop fusion | bytes 5242880 | tf_op jit(solution)/shard_map/squeeze | solution.py:123
  154.9 11.0 %collective-permute-start.18 = (f32[3,34,1]{2,1,0:T(8,128)}, f32[3,34,1]{2,1,0:T(8,128)}, u32[]{:S(2)}, u32[]{:S(2)}) collective-permute-start(f32[3,34,1]{2,1,0:T(8,128)} %get-tuple-element.218), channel_id=1, source_target_pairs={{0,1},{1,2},{2,3},{3,4},{4,5},{5,6},{6,7},{7,8},{8,9},{9,10},{10,1... | collective-permute-start | bytes 1232 | tf_op jit(solution)/shard_map/ppermute | solution.py:33
  166.1 1.4 pad_maximum_fusion.1
  167.5 3.7 %fusion.149 = (f32[2,80,34,1]{3,2,1,0:T(8,128)}, f32[2,80,34,1]{3,2,1,0:T(8,128)}) fusion(f32[2,80,34,128]{3,2,1,0:T(8,128)S(1)} %pad_maximum_fusion.1), kind=kLoop, calls=%fused_computation.407 | loop fusion | bytes 87040 | tf_op jit(solution)/shard_map/slice | solution.py:30
  171.2 2.9 copy.121
  175.4 3.4 copy.119
  178.9 7.0 %collective-permute-start.19 = (f32[2,80,34,1]{1,0,3,2:T(2,128)}, f32[2,80,34,1]{1,0,3,2:T(2,128)}, u32[]{:S(2)}, u32[]{:S(2)}) collective-permute-start(f32[2,80,34,1]{1,0,3,2:T(2,128)} %copy.119), channel_id=1, source_target_pairs={{0,1},{1,2},{2,3},{3,4},{4,5},{5,6},{6,7},{7,8},{8,9},{9,10},{10,1... | collective-permute-start | bytes 65288 | tf_op jit(solution)/shard_map/ppermute | solution.py:33
  186.7 3.2 copy.122
  189.9 3.1 copy.120
  193.0 7.1 %fusion.52 = f32[2,80,32,128]{3,2,1,0:T(8,128)S(1)} fusion(f32[2,80,34,1]{3,2,1,0:T(8,128)} %copy.122, f32[2,80,1,128]{3,2,1,0:T(1,128)} %copy-done.41, f32[2,80,1,128]{3,2,1,0:T(1,128)} %collective-permute-done.15, f32[1,80,32,128]{3,2,1,0:T(8,128)S(1)} %bitcast.328, f32[1,80,32,128]{3,2,1,0:T(8,128)S(1)} %bitcast.324, f32[2,80,34,1]{3,2,1,0:T(8,128)} %copy.120, ...), kind=kLoop, calls=%fused_computation.95 | loop fusion | flops 18350080 | bytes 8120832 | tf_op jit(solution)/shard_map/add | solution.py:191
  200.7 1.3 collective-permute-start.23
  202.0 4.6 %collective-permute-start.22 = (f32[2,80,1,128]{3,2,1,0:T(1,128)S(1)}, f32[2,80,1,128]{3,2,1,0:T(1,128)S(1)}, u32[]{:S(2)}, u32[]{:S(2)}) collective-permute-start(f32[2,80,1,128]{3,2,1,0:T(1,128)S(1)} %get-tuple-element.194), channel_id=1, source_target_pairs={{0,16},{16,32},{32,48},{48,64},{64,80},{80,96},{96,112},{1,17},{17... | collective-permute-start | bytes 245768 | tf_op jit(solution)/shard_map/ppermute | solution.py:33
  209.7 3.7 %fusion.148 = (f32[2,80,34,1]{3,2,1,0:T(8,128)}, f32[2,80,34,1]{3,2,1,0:T(8,128)}) fusion(f32[2,80,34,128]{3,2,1,0:T(8,128)S(1)} %pad_maximum_fusion.2), kind=kLoop, calls=%fused_computation.406 | loop fusion | bytes 87040 | tf_op jit(solution)/shard_map/slice | solution.py:30
  213.4 2.9 copy.125
  217.6 3.4 copy.123
  221.1 4.9 %collective-permute-start.24 = (f32[2,80,34,1]{1,0,3,2:T(2,128)}, f32[2,80,34,1]{1,0,3,2:T(2,128)}, u32[]{:S(2)}, u32[]{:S(2)}) collective-permute-start(f32[2,80,34,1]{1,0,3,2:T(2,128)} %copy.123), channel_id=1, source_target_pairs={{0,1},{1,2},{2,3},{3,4},{4,5},{5,6},{6,7},{7,8},{8,9},{9,10},{10,1... | collective-permute-start | bytes 65288 | tf_op jit(solution)/shard_map/ppermute | solution.py:33
  226.0 1.9 fusion.67
  227.9 3.2 copy.126
  231.0 3.1 copy.124
  234.2 8.7 %fusion.39 = f32[2,80,32,128]{3,2,1,0:T(8,128)S(1)} fusion(f32[2,80,32,128]{3,2,1,0:T(8,128)S(1)} %bitcast_dynamic-update-slice_fusion.6, f32[2,80,34,1]{3,2,1,0:T(8,128)} %copy.126, f32[2,80,1,128]{3,2,1,0:T(1,128)} %copy-done.48, f32[2,80,1,128]{3,2,1,0:T(1,128)} %copy-done.51, f32[2,80,34,1]{3,2,1,0:T(8,128)} %copy.124, f32[2,79,32,128]{3,2,1,0:T(8,128)} %fusion.67, ...), kind=kLoop, calls=%fused_computation.74 | loop fusion | flops 15073280 | bytes 8120832 | tf_op jit(solution)/shard_map/add | solution.py:191
  244.6 5.8 %collective-permute-start.26 = (f32[2,80,1,128]{3,2,1,0:T(1,128)S(1)}, f32[2,80,1,128]{3,2,1,0:T(1,128)S(1)}, u32[]{:S(2)}, u32[]{:S(2)}) collective-permute-start(f32[2,80,1,128]{3,2,1,0:T(1,128)S(1)} %get-tuple-element.192), channel_id=1, source_target_pairs={{0,16},{16,32},{32,48},{48,64},{64,80},{80,96},{96,112},{1,17},{17... | collective-permute-start | bytes 245768 | tf_op jit(solution)/shard_map/ppermute | solution.py:33
  253.6 3.7 %fusion.147 = (f32[2,80,34,1]{3,2,1,0:T(8,128)}, f32[2,80,34,1]{3,2,1,0:T(8,128)}) fusion(f32[2,80,34,128]{3,2,1,0:T(8,128)S(1)} %pad_maximum_fusion.3), kind=kLoop, calls=%fused_computation.405 | loop fusion | bytes 87040 | tf_op jit(solution)/shard_map/slice | solution.py:30
  257.3 2.9 copy.129
  261.5 2.9 copy.127
  264.5 4.8 %collective-permute-start.28 = (f32[2,80,34,1]{1,0,3,2:T(2,128)S(1)}, f32[2,80,34,1]{1,0,3,2:T(2,128)S(1)}, u32[]{:S(2)}, u32[]{:S(2)}) collective-permute-start(f32[2,80,34,1]{1,0,3,2:T(2,128)S(1)} %copy.127), channel_id=1, source_target_pairs={{0,1},{1,2},{2,3},{3,4},{4,5},{5,6},{6,7},{7,8},{8,9},{9,10},{10,1... | collective-permute-start | bytes 65288 | tf_op jit(solution)/shard_map/ppermute | solution.py:33
  269.3 1.9 fusion.66
  271.2 2.5 copy.130
  273.7 2.5 copy.128
  276.3 8.6 %fusion.26 = f32[2,80,32,128]{3,2,1,0:T(8,128)S(1)} fusion(f32[2,80,32,128]{3,2,1,0:T(8,128)S(1)} %bitcast_dynamic-update-slice_fusion.4, f32[2,80,34,1]{3,2,1,0:T(8,128)} %copy.130, f32[2,80,1,128]{3,2,1,0:T(1,128)S(1)} %copy-done.47, f32[2,80,1,128]{3,2,1,0:T(1,128)S(1)} %copy-done.50, f32[2,80,34,1]{3,2,1,0:T(8,128)} %copy.128, ...), kind=kLoop, calls=%fused_computation.53 | loop fusion | flops 15073280 | bytes 8120832 | tf_op jit(solution)/shard_map/add | solution.py:191
  285.4 1.4 collective-permute-start.31
  286.8 6.9 %collective-permute-start.30 = (f32[2,80,1,128]{3,2,1,0:T(1,128)S(1)}, f32[2,80,1,128]{3,2,1,0:T(1,128)S(1)}, u32[]{:S(2)}, u32[]{:S(2)}) collective-permute-start(f32[2,80,1,128]{3,2,1,0:T(1,128)S(1)} %get-tuple-element.190), channel_id=1, source_target_pairs={{0,16},{16,32},{32,48},{48,64},{64,80},{80,96},{96,112},{1,17},{17... | collective-permute-start | bytes 245768 | tf_op jit(solution)/shard_map/ppermute | solution.py:33
  296.7 3.7 %fusion.146 = (f32[2,80,34,1]{3,2,1,0:T(8,128)}, f32[2,80,34,1]{3,2,1,0:T(8,128)}) fusion(f32[2,80,34,128]{3,2,1,0:T(8,128)S(1)} %pad_maximum_fusion.4), kind=kLoop, calls=%fused_computation.404 | loop fusion | bytes 87040 | tf_op jit(solution)/shard_map/slice | solution.py:30
  300.4 2.9 copy.133
  304.6 2.9 copy.131
  307.5 6.4 %collective-permute-start.32 = (f32[2,80,34,1]{1,0,3,2:T(2,128)S(1)}, f32[2,80,34,1]{1,0,3,2:T(2,128)S(1)}, u32[]{:S(2)}, u32[]{:S(2)}) collective-permute-start(f32[2,80,34,1]{1,0,3,2:T(2,128)S(1)} %copy.131), channel_id=1, source_target_pairs={{0,1},{1,2},{2,3},{3,4},{4,5},{5,6},{6,7},{7,8},{8,9},{9,10},{10,1... | collective-permute-start | bytes 65288 | tf_op jit(solution)/shard_map/ppermute | solution.py:33
  313.9 1.9 fusion.65
  315.8 2.5 copy.134
  318.3 2.5 copy.132
  320.8 8.6 %fusion.13 = f32[2,80,32,128]{3,2,1,0:T(8,128)S(1)} fusion(f32[2,80,32,128]{3,2,1,0:T(8,128)S(1)} %bitcast_dynamic-update-slice_fusion.2, f32[2,80,34,1]{3,2,1,0:T(8,128)} %copy.134, f32[2,80,1,128]{3,2,1,0:T(1,128)S(1)} %copy-done.43, f32[2,80,1,128]{3,2,1,0:T(1,128)S(1)} %copy-done.45, f32[2,80,34,1]{3,2,1,0:T(8,128)} %copy.132, ...), kind=kLoop, calls=%fused_computation.32 | loop fusion | flops 15073280 | bytes 8120832 | tf_op jit(solution)/shard_map/add | solution.py:191
  331.1 27.1 %all-to-all-start.1 = ((f32[128,1,128]{2,1,0:T(1,128)}), f32[128,1,128]{2,1,0:T(1,128)S(1)}, u32[]{:S(2)}, u32[]{:S(2)}) async-start(f32[128,1,128]{2,1,0:T(1,128)} %bitcast.114), calls=%async_computation.1 | async-start | bytes 131072 | tf_op jit(solution)/shard_map/all_to_all | solution.py:281
  358.2 1.7 slice_bitcast_fusion
  359.9 7.4 %all-to-all-done.1 = f32[128,1,128]{2,1,0:T(1,128)S(1)} async-done(((f32[128,1,128]{2,1,0:T(1,128)}), f32[128,1,128]{2,1,0:T(1,128)S(1)}, u32[]{:S(2)}, u32[]{:S(2)}) %all-to-all-start.1) | async-done | bytes 65568 | tf_op jit(solution)/shard_map/all_to_all | solution.py:281
  (304 shorter events, 48.2 us)
Async XLA Ops:
  0.6 16.2 %copy-start = (f32[16,16]{1,0:T(8,128)S(1)}, f32[16,16]{1,0:T(8,128)}, u32[]{:S(2)}) copy-start(f32[16,16]{1,0:T(8,128)} %constant.260.clone) | copy-start | bytes 3076
  0.6 14.2 %copy-start.64 = (s32[32]{0:T(128)S(1)}, s32[32]{0:T(128)}, u32[]{:S(2)}) copy-start(s32[32]{0:T(128)} %param.38) | copy-start | bytes 388
  0.7 14.2 %copy-start.65 = (s32[32]{0:T(128)S(1)}, s32[32]{0:T(128)}, u32[]{:S(2)}) copy-start(s32[32]{0:T(128)} %param.33) | copy-start | bytes 388
  0.7 14.7 %copy-start.56 = (f32[32,128]{1,0:T(8,128)S(1)}, f32[32,128]{1,0:T(8,128)}, u32[]{:S(2)}) copy-start(f32[32,128]{1,0:T(8,128)} %param.30) | copy-start | bytes 49156
  2.4 13.0 %collective-permute-start = (f32[10,1,128]{2,1,0:T(1,128)S(1)}, f32[10,1,128]{2,1,0:T(1,128)S(1)}, u32[]{:S(2)}, u32[]{:S(2)}) collective-permute-start(f32[10,1,128]{2,1,0:T(1,128)S(1)} %slice.1076), channel_id=1, source_target_pairs={{0,16},{16,32},{32,48},{48,64},{64,80},{80,96},{96,112},{1,17},{17... | collective-permute-start | bytes 15368 | tf_op jit(solution)/shard_map/ppermute | solution.py:45
  8.4 157.7 %collective-permute-start.17 = (f32[2,80,1,128]{3,2,1,0:T(1,128)}, f32[2,80,1,128]{3,2,1,0:T(1,128)S(1)}, u32[]{:S(2)}, u32[]{:S(2)}) collective-permute-start(f32[2,80,1,128]{3,2,1,0:T(1,128)} %get-tuple-element.197), channel_id=1, source_target_pairs={{16,0},{32,16},{48,32},{64,48},{80,64},{96,80},{112,96},{17,1},{33... | collective-permute-start | bytes 245768 | tf_op jit(solution)/shard_map/ppermute | solution.py:35
  9.6 156.5 %collective-permute-start.15 = (f32[2,80,1,128]{3,2,1,0:T(1,128)}, f32[2,80,1,128]{3,2,1,0:T(1,128)}, u32[]{:S(2)}, u32[]{:S(2)}) collective-permute-start(f32[2,80,1,128]{3,2,1,0:T(1,128)} %get-tuple-element.196), channel_id=1, source_target_pairs={{0,16},{16,32},{32,48},{48,64},{64,80},{80,96},{96,112},{1,17},{17... | collective-permute-start | bytes 245768 | tf_op jit(solution)/shard_map/ppermute | solution.py:33
  15.4 36.1 %copy-start.4 = (f32[11,32,128]{2,1,0:T(8,128)}, f32[11,32,128]{2,1,0:T(8,128)S(1)}, u32[]{:S(2)}) copy-start(f32[11,32,128]{2,1,0:T(8,128)S(1)} %pad_add_fusion) | copy-start | bytes 540676
  15.5 2.4 collective-permute-start.1
  19.6 31.9 %copy-start.7 = (f32[1,11,32,128]{3,2,1,0:T(8,128)}, f32[1,11,32,128]{3,2,1,0:T(8,128)S(1)}, u32[]{:S(2)}) copy-start(f32[1,11,32,128]{3,2,1,0:T(8,128)S(1)} %get-tuple-element.227) | copy-start | bytes 540676
  19.6 31.9 %copy-start.10 = (f32[1,11,32,128]{3,2,1,0:T(8,128)}, f32[1,11,32,128]{3,2,1,0:T(8,128)S(1)}, u32[]{:S(2)}) copy-start(f32[1,11,32,128]{3,2,1,0:T(8,128)S(1)} %get-tuple-element.228) | copy-start | bytes 540676
  20.4 5.9 %collective-permute-start.3 = (f32[2,11,1,128]{3,2,1,0:T(1,128)S(1)}, f32[2,11,1,128]{3,2,1,0:T(1,128)S(1)}, u32[]{:S(2)}, u32[]{:S(2)}) collective-permute-start(f32[2,11,1,128]{3,2,1,0:T(1,128)S(1)} %get-tuple-element.215), channel_id=1, source_target_pairs={{16,0},{32,16},{48,32},{64,48},{80,64},{96,80},{112,96},{17,1},{33... | collective-permute-start | bytes 33800 | tf_op jit(solution)/shard_map/ppermute | solution.py:35
  21.7 5.9 %collective-permute-start.2 = (f32[2,11,1,128]{3,2,1,0:T(1,128)S(1)}, f32[2,11,1,128]{3,2,1,0:T(1,128)S(1)}, u32[]{:S(2)}, u32[]{:S(2)}) collective-permute-start(f32[2,11,1,128]{3,2,1,0:T(1,128)S(1)} %get-tuple-element.214), channel_id=1, source_target_pairs={{0,16},{16,32},{32,48},{48,64},{64,80},{80,96},{96,112},{1,17},{17... | collective-permute-start | bytes 33800 | tf_op jit(solution)/shard_map/ppermute | solution.py:33
  26.2 31.3 %copy-start.58 = (pred[32]{0:T(512)(128)(4,1)}, pred[32]{0:T(512)(128)(4,1)S(1)}, u32[]{:S(2)}) copy-start(pred[32]{0:T(512)(128)(4,1)S(1)} %broadcast_compare_fusion) | copy-start | bytes 100
  27.8 8.8 %collective-permute-start.5 = (f32[2,11,34,1]{3,2,1,0:T(8,128)S(1)}, f32[2,11,34,1]{3,2,1,0:T(8,128)S(1)}, u32[]{:S(2)}, u32[]{:S(2)}) collective-permute-start(f32[2,11,34,1]{3,2,1,0:T(8,128)S(1)} %get-tuple-element.202), channel_id=1, source_target_pairs={{1,0},{2,1},{3,2},{4,3},{5,4},{6,5},{7,6},{8,7},{9,8},{10,9},{11,1... | collective-permute-start | bytes 8984 | tf_op jit(solution)/shard_map/ppermute | solution.py:35
  29.1 8.2 %collective-permute-start.4 = (f32[2,11,34,1]{3,2,1,0:T(8,128)S(1)}, f32[2,11,34,1]{3,2,1,0:T(8,128)S(1)}, u32[]{:S(2)}, u32[]{:S(2)}) collective-permute-start(f32[2,11,34,1]{3,2,1,0:T(8,128)S(1)} %get-tuple-element.203), channel_id=1, source_target_pairs={{0,1},{1,2},{2,3},{3,4},{4,5},{5,6},{6,7},{7,8},{8,9},{9,10},{10,1... | collective-permute-start | bytes 8984 | tf_op jit(solution)/shard_map/ppermute | solution.py:33
  36.7 20.9 %copy-start.62 = (s32[32]{0:T(128)}, s32[32]{0:T(128)S(1)}, u32[]{:S(2)}) copy-start(s32[32]{0:T(128)S(1)} %add.564) | copy-start | bytes 388
  51.3 35.0 %copy-start.13 = (f32[1,11,32,128]{3,2,1,0:T(8,128)}, f32[1,11,32,128]{3,2,1,0:T(8,128)S(1)}, u32[]{:S(2)}) copy-start(f32[1,11,32,128]{3,2,1,0:T(8,128)S(1)} %add_bitcast_fusion.4) | copy-start | bytes 540676
  51.5 41.0 %copy-start.16 = (f32[1,11,32,128]{3,2,1,0:T(8,128)}, f32[1,11,32,128]{3,2,1,0:T(8,128)S(1)}, u32[]{:S(2)}) copy-start(f32[1,11,32,128]{3,2,1,0:T(8,128)S(1)} %add_bitcast_fusion.5) | copy-start | bytes 540676
  51.5 39.2 %copy-start.23 = (s32[32,128]{1,0:T(8,128)S(1)}, s32[32,128]{1,0:T(8,128)}, u32[]{:S(2)}) copy-start(s32[32,128]{1,0:T(8,128)} %param.37) | copy-start | bytes 49156
  51.7 34.3 %collective-permute-start.7 = (f32[2,11,1,128]{3,2,1,0:T(1,128)S(1)}, f32[2,11,1,128]{3,2,1,0:T(1,128)S(1)}, u32[]{:S(2)}, u32[]{:S(2)}) collective-permute-start(f32[2,11,1,128]{3,2,1,0:T(1,128)S(1)} %get-tuple-element.213), channel_id=1, source_target_pairs={{16,0},{32,16},{48,32},{64,48},{80,64},{96,80},{112,96},{17,1},{33... | collective-permute-start | bytes 33800 | tf_op jit(solution)/shard_map/ppermute | solution.py:35
  53.0 33.0 %collective-permute-start.6 = (f32[2,11,1,128]{3,2,1,0:T(1,128)S(1)}, f32[2,11,1,128]{3,2,1,0:T(1,128)S(1)}, u32[]{:S(2)}, u32[]{:S(2)}) collective-permute-start(f32[2,11,1,128]{3,2,1,0:T(1,128)S(1)} %get-tuple-element.212), channel_id=1, source_target_pairs={{0,16},{16,32},{32,48},{48,64},{64,80},{80,96},{96,112},{1,17},{17... | collective-permute-start | bytes 33800 | tf_op jit(solution)/shard_map/ppermute | solution.py:33
  58.4 83.4 %all-to-all-start = ((f32[128,1,128]{2,1,0:T(1,128)}), f32[128,1,128]{2,1,0:T(1,128)}, u32[]{:S(2)}, u32[]{:S(2)}) async-start(f32[128,1,128]{2,1,0:T(1,128)} %bitcast.85), calls=%async_computation | async-start | bytes 131072 | tf_op jit(solution)/shard_map/all_to_all | solution.py:258
  86.3 4.4 %collective-permute-start.9 = (f32[2,11,34,1]{3,2,1,0:T(8,128)S(1)}, f32[2,11,34,1]{3,2,1,0:T(8,128)S(1)}, u32[]{:S(2)}, u32[]{:S(2)}) collective-permute-start(f32[2,11,34,1]{3,2,1,0:T(8,128)S(1)} %get-tuple-element.200), channel_id=1, source_target_pairs={{1,0},{2,1},{3,2},{4,3},{5,4},{6,5},{7,6},{8,7},{9,8},{10,9},{11,1... | collective-permute-start | bytes 8984 | tf_op jit(solution)/shard_map/ppermute | solution.py:35
  87.6 4.5 %collective-permute-start.8 = (f32[2,11,34,1]{3,2,1,0:T(8,128)S(1)}, f32[2,11,34,1]{3,2,1,0:T(8,128)S(1)}, u32[]{:S(2)}, u32[]{:S(2)}) collective-permute-start(f32[2,11,34,1]{3,2,1,0:T(8,128)S(1)} %get-tuple-element.201), channel_id=1, source_target_pairs={{0,1},{1,2},{2,3},{3,4},{4,5},{5,6},{6,7},{7,8},{8,9},{9,10},{10,1... | collective-permute-start | bytes 8984 | tf_op jit(solution)/shard_map/ppermute | solution.py:33
  107.5 7.8 %collective-permute-start.11 = (f32[2,11,1,128]{3,2,1,0:T(1,128)S(1)}, f32[2,11,1,128]{3,2,1,0:T(1,128)S(1)}, u32[]{:S(2)}, u32[]{:S(2)}) collective-permute-start(f32[2,11,1,128]{3,2,1,0:T(1,128)S(1)} %get-tuple-element.211), channel_id=1, source_target_pairs={{16,0},{32,16},{48,32},{64,48},{80,64},{96,80},{112,96},{17,1},{33... | collective-permute-start | bytes 33800 | tf_op jit(solution)/shard_map/ppermute | solution.py:35
  108.7 6.5 %collective-permute-start.10 = (f32[2,11,1,128]{3,2,1,0:T(1,128)S(1)}, f32[2,11,1,128]{3,2,1,0:T(1,128)S(1)}, u32[]{:S(2)}, u32[]{:S(2)}) collective-permute-start(f32[2,11,1,128]{3,2,1,0:T(1,128)S(1)} %get-tuple-element.210), channel_id=1, source_target_pairs={{0,16},{16,32},{32,48},{48,64},{64,80},{80,96},{96,112},{1,17},{17... | collective-permute-start | bytes 33800 | tf_op jit(solution)/shard_map/ppermute | solution.py:33
  115.2 9.6 %copy-start.57 = (s32[32]{0:T(128)S(1)}, s32[32]{0:T(128)}, u32[]{:S(2)}) copy-start(s32[32]{0:T(128)} %get-tuple-element.224) | copy-start | bytes 388
  115.5 10.1 %collective-permute-start.13 = (f32[2,11,34,1]{3,2,1,0:T(8,128)S(1)}, f32[2,11,34,1]{3,2,1,0:T(8,128)S(1)}, u32[]{:S(2)}, u32[]{:S(2)}) collective-permute-start(f32[2,11,34,1]{3,2,1,0:T(8,128)S(1)} %get-tuple-element.198), channel_id=1, source_target_pairs={{1,0},{2,1},{3,2},{4,3},{5,4},{6,5},{7,6},{8,7},{9,8},{10,9},{11,1... | collective-permute-start | bytes 8984 | tf_op jit(solution)/shard_map/ppermute | solution.py:35
  116.8 9.5 %collective-permute-start.12 = (f32[2,11,34,1]{3,2,1,0:T(8,128)S(1)}, f32[2,11,34,1]{3,2,1,0:T(8,128)S(1)}, u32[]{:S(2)}, u32[]{:S(2)}) collective-permute-start(f32[2,11,34,1]{3,2,1,0:T(8,128)S(1)} %get-tuple-element.199), channel_id=1, source_target_pairs={{0,1},{1,2},{2,3},{3,4},{4,5},{5,6},{6,7},{7,8},{8,9},{9,10},{10,1... | collective-permute-start | bytes 8984 | tf_op jit(solution)/shard_map/ppermute | solution.py:33
  142.9 10.0 %collective-permute-start.16 = (f32[3,1,128]{2,1,0:T(1,128)S(1)}, f32[3,1,128]{2,1,0:T(1,128)S(1)}, u32[]{:S(2)}, u32[]{:S(2)}) collective-permute-start(f32[3,1,128]{2,1,0:T(1,128)S(1)} %get-tuple-element.221), channel_id=1, source_target_pairs={{16,0},{32,16},{48,32},{64,48},{80,64},{96,80},{112,96},{17,1},{33... | collective-permute-start | bytes 4616 | tf_op jit(solution)/shard_map/ppermute | solution.py:35
  144.2 8.7 %collective-permute-start.14 = (f32[3,1,128]{2,1,0:T(1,128)S(1)}, f32[3,1,128]{2,1,0:T(1,128)S(1)}, u32[]{:S(2)}, u32[]{:S(2)}) collective-permute-start(f32[3,1,128]{2,1,0:T(1,128)S(1)} %get-tuple-element.220), channel_id=1, source_target_pairs={{0,16},{16,32},{32,48},{48,64},{64,80},{80,96},{96,112},{1,17},{17... | collective-permute-start | bytes 4616 | tf_op jit(solution)/shard_map/ppermute | solution.py:33
  153.6 12.4 %collective-permute-start.20 = (f32[3,34,1]{2,1,0:T(8,128)S(1)}, f32[3,34,1]{2,1,0:T(8,128)S(1)}, u32[]{:S(2)}, u32[]{:S(2)}) collective-permute-start(f32[3,34,1]{2,1,0:T(8,128)S(1)} %get-tuple-element.219), channel_id=1, source_target_pairs={{1,0},{2,1},{3,2},{4,3},{5,4},{6,5},{7,6},{8,7},{9,8},{10,9},{11,1... | collective-permute-start | bytes 1232 | tf_op jit(solution)/shard_map/ppermute | solution.py:35
  154.9 31.0 %collective-permute-start.18 = (f32[3,34,1]{2,1,0:T(8,128)}, f32[3,34,1]{2,1,0:T(8,128)}, u32[]{:S(2)}, u32[]{:S(2)}) collective-permute-start(f32[3,34,1]{2,1,0:T(8,128)} %get-tuple-element.218), channel_id=1, source_target_pairs={{0,1},{1,2},{2,3},{3,4},{4,5},{5,6},{6,7},{7,8},{8,9},{9,10},{10,1... | collective-permute-start | bytes 1232 | tf_op jit(solution)/shard_map/ppermute | solution.py:33
  174.1 12.6 %collective-permute-start.21 = (f32[2,80,34,1]{1,0,3,2:T(2,128)S(1)}, f32[2,80,34,1]{1,0,3,2:T(2,128)}, u32[]{:S(2)}, u32[]{:S(2)}) collective-permute-start(f32[2,80,34,1]{1,0,3,2:T(2,128)S(1)} %copy.121), channel_id=1, source_target_pairs={{1,0},{2,1},{3,2},{4,3},{5,4},{6,5},{7,6},{8,7},{9,8},{10,9},{11,1... | collective-permute-start | bytes 65288 | tf_op jit(solution)/shard_map/ppermute | solution.py:35
  178.9 11.0 %collective-permute-start.19 = (f32[2,80,34,1]{1,0,3,2:T(2,128)}, f32[2,80,34,1]{1,0,3,2:T(2,128)}, u32[]{:S(2)}, u32[]{:S(2)}) collective-permute-start(f32[2,80,34,1]{1,0,3,2:T(2,128)} %copy.119), channel_id=1, source_target_pairs={{0,1},{1,2},{2,3},{3,4},{4,5},{5,6},{6,7},{7,8},{8,9},{9,10},{10,1... | collective-permute-start | bytes 65288 | tf_op jit(solution)/shard_map/ppermute | solution.py:33
  200.7 6.7 %collective-permute-start.23 = (f32[2,80,1,128]{3,2,1,0:T(1,128)S(1)}, f32[2,80,1,128]{3,2,1,0:T(1,128)S(1)}, u32[]{:S(2)}, u32[]{:S(2)}) collective-permute-start(f32[2,80,1,128]{3,2,1,0:T(1,128)S(1)} %get-tuple-element.195), channel_id=1, source_target_pairs={{16,0},{32,16},{48,32},{64,48},{80,64},{96,80},{112,96},{17,1},{33... | collective-permute-start | bytes 245768 | tf_op jit(solution)/shard_map/ppermute | solution.py:35
  202.0 6.6 %collective-permute-start.22 = (f32[2,80,1,128]{3,2,1,0:T(1,128)S(1)}, f32[2,80,1,128]{3,2,1,0:T(1,128)S(1)}, u32[]{:S(2)}, u32[]{:S(2)}) collective-permute-start(f32[2,80,1,128]{3,2,1,0:T(1,128)S(1)} %get-tuple-element.194), channel_id=1, source_target_pairs={{0,16},{16,32},{32,48},{48,64},{64,80},{80,96},{96,112},{1,17},{17... | collective-permute-start | bytes 245768 | tf_op jit(solution)/shard_map/ppermute | solution.py:33
  216.3 11.6 %collective-permute-start.25 = (f32[2,80,34,1]{1,0,3,2:T(2,128)S(1)}, f32[2,80,34,1]{1,0,3,2:T(2,128)}, u32[]{:S(2)}, u32[]{:S(2)}) collective-permute-start(f32[2,80,34,1]{1,0,3,2:T(2,128)S(1)} %copy.125), channel_id=1, source_target_pairs={{1,0},{2,1},{3,2},{4,3},{5,4},{6,5},{7,6},{8,7},{9,8},{10,9},{11,1... | collective-permute-start | bytes 65288 | tf_op jit(solution)/shard_map/ppermute | solution.py:35
  221.1 10.0 %collective-permute-start.24 = (f32[2,80,34,1]{1,0,3,2:T(2,128)}, f32[2,80,34,1]{1,0,3,2:T(2,128)}, u32[]{:S(2)}, u32[]{:S(2)}) collective-permute-start(f32[2,80,34,1]{1,0,3,2:T(2,128)} %copy.123), channel_id=1, source_target_pairs={{0,1},{1,2},{2,3},{3,4},{4,5},{5,6},{6,7},{7,8},{8,9},{9,10},{10,1... | collective-permute-start | bytes 65288 | tf_op jit(solution)/shard_map/ppermute | solution.py:33
  242.9 7.6 %copy-start.27 = (f32[10,32,128]{2,1,0:T(8,128)S(1)}, f32[10,32,128]{2,1,0:T(8,128)}, u32[]{:S(2)}) copy-start(f32[10,32,128]{2,1,0:T(8,128)} %get-tuple-element.126) | copy-start | bytes 491524
  242.9 7.6 %copy-start.28 = (f32[10,32,128]{2,1,0:T(8,128)S(1)}, f32[10,32,128]{2,1,0:T(8,128)}, u32[]{:S(2)}) copy-start(f32[10,32,128]{2,1,0:T(8,128)} %get-tuple-element.127) | copy-start | bytes 491524
  243.3 7.9 %collective-permute-start.27 = (f32[2,80,1,128]{3,2,1,0:T(1,128)S(1)}, f32[2,80,1,128]{3,2,1,0:T(1,128)S(1)}, u32[]{:S(2)}, u32[]{:S(2)}) collective-permute-start(f32[2,80,1,128]{3,2,1,0:T(1,128)S(1)} %get-tuple-element.193), channel_id=1, source_target_pairs={{16,0},{32,16},{48,32},{64,48},{80,64},{96,80},{112,96},{17,1},{33... | collective-permute-start | bytes 245768 | tf_op jit(solution)/shard_map/ppermute | solution.py:35
  244.6 7.8 %collective-permute-start.26 = (f32[2,80,1,128]{3,2,1,0:T(1,128)S(1)}, f32[2,80,1,128]{3,2,1,0:T(1,128)S(1)}, u32[]{:S(2)}, u32[]{:S(2)}) collective-permute-start(f32[2,80,1,128]{3,2,1,0:T(1,128)S(1)} %get-tuple-element.192), channel_id=1, source_target_pairs={{0,16},{16,32},{32,48},{48,64},{64,80},{80,96},{96,112},{1,17},{17... | collective-permute-start | bytes 245768 | tf_op jit(solution)/shard_map/ppermute | solution.py:33
  260.2 11.0 %collective-permute-start.29 = (f32[2,80,34,1]{1,0,3,2:T(2,128)S(1)}, f32[2,80,34,1]{1,0,3,2:T(2,128)S(1)}, u32[]{:S(2)}, u32[]{:S(2)}) collective-permute-start(f32[2,80,34,1]{1,0,3,2:T(2,128)S(1)} %copy.129), channel_id=1, source_target_pairs={{1,0},{2,1},{3,2},{4,3},{5,4},{6,5},{7,6},{8,7},{9,8},{10,9},{11,1... | collective-permute-start | bytes 65288 | tf_op jit(solution)/shard_map/ppermute | solution.py:35
  264.5 9.3 %collective-permute-start.28 = (f32[2,80,34,1]{1,0,3,2:T(2,128)S(1)}, f32[2,80,34,1]{1,0,3,2:T(2,128)S(1)}, u32[]{:S(2)}, u32[]{:S(2)}) collective-permute-start(f32[2,80,34,1]{1,0,3,2:T(2,128)S(1)} %copy.127), channel_id=1, source_target_pairs={{0,1},{1,2},{2,3},{3,4},{4,5},{5,6},{6,7},{7,8},{8,9},{9,10},{10,1... | collective-permute-start | bytes 65288 | tf_op jit(solution)/shard_map/ppermute | solution.py:33
  284.9 8.9 %copy-start.6 = (f32[11,32,128]{2,1,0:T(8,128)S(1)}, f32[11,32,128]{2,1,0:T(8,128)}, u32[]{:S(2)}) copy-start(f32[11,32,128]{2,1,0:T(8,128)} %copy-done.4) | copy-start | bytes 540676
  284.9 8.9 %copy-start.9 = (f32[1,11,32,128]{3,2,1,0:T(8,128)S(1)}, f32[1,11,32,128]{3,2,1,0:T(8,128)}, u32[]{:S(2)}) copy-start(f32[1,11,32,128]{3,2,1,0:T(8,128)} %copy-done.7) | copy-start | bytes 540676
  284.9 8.9 %copy-start.12 = (f32[1,11,32,128]{3,2,1,0:T(8,128)S(1)}, f32[1,11,32,128]{3,2,1,0:T(8,128)}, u32[]{:S(2)}) copy-start(f32[1,11,32,128]{3,2,1,0:T(8,128)} %copy-done.10) | copy-start | bytes 540676
  284.9 8.9 %copy-start.15 = (f32[1,11,32,128]{3,2,1,0:T(8,128)S(1)}, f32[1,11,32,128]{3,2,1,0:T(8,128)}, u32[]{:S(2)}) copy-start(f32[1,11,32,128]{3,2,1,0:T(8,128)} %copy-done.13) | copy-start | bytes 540676
  284.9 8.9 %copy-start.18 = (f32[1,11,32,128]{3,2,1,0:T(8,128)S(1)}, f32[1,11,32,128]{3,2,1,0:T(8,128)}, u32[]{:S(2)}) copy-start(f32[1,11,32,128]{3,2,1,0:T(8,128)} %copy-done.16) | copy-start | bytes 540676
  284.9 8.9 %copy-start.20 = (f32[1,11,32,128]{3,2,1,0:T(8,128)S(1)}, f32[1,11,32,128]{3,2,1,0:T(8,128)}, u32[]{:S(2)}) copy-start(f32[1,11,32,128]{3,2,1,0:T(8,128)} %copy-done.19) | copy-start | bytes 540676
  284.9 8.9 %copy-start.22 = (f32[1,11,32,128]{3,2,1,0:T(8,128)S(1)}, f32[1,11,32,128]{3,2,1,0:T(8,128)}, u32[]{:S(2)}) copy-start(f32[1,11,32,128]{3,2,1,0:T(8,128)} %copy-done.21) | copy-start | bytes 540676
  284.9 8.9 %copy-start.25 = (f32[1,11,32,128]{3,2,1,0:T(8,128)S(1)}, f32[1,11,32,128]{3,2,1,0:T(8,128)}, u32[]{:S(2)}) copy-start(f32[1,11,32,128]{3,2,1,0:T(8,128)} %add_bitcast_fusion) | copy-start | bytes 540676
  285.0 8.9 %copy-start.26 = (f32[1,11,32,128]{3,2,1,0:T(8,128)S(1)}, f32[1,11,32,128]{3,2,1,0:T(8,128)}, u32[]{:S(2)}) copy-start(f32[1,11,32,128]{3,2,1,0:T(8,128)} %add_bitcast_fusion.1) | copy-start | bytes 540676
  285.4 9.5 %collective-permute-start.31 = (f32[2,80,1,128]{3,2,1,0:T(1,128)S(1)}, f32[2,80,1,128]{3,2,1,0:T(1,128)S(1)}, u32[]{:S(2)}, u32[]{:S(2)}) collective-permute-start(f32[2,80,1,128]{3,2,1,0:T(1,128)S(1)} %get-tuple-element.191), channel_id=1, source_target_pairs={{16,0},{32,16},{48,32},{64,48},{80,64},{96,80},{112,96},{17,1},{33... | collective-permute-start | bytes 245768 | tf_op jit(solution)/shard_map/ppermute | solution.py:35
  286.8 8.7 %collective-permute-start.30 = (f32[2,80,1,128]{3,2,1,0:T(1,128)S(1)}, f32[2,80,1,128]{3,2,1,0:T(1,128)S(1)}, u32[]{:S(2)}, u32[]{:S(2)}) collective-permute-start(f32[2,80,1,128]{3,2,1,0:T(1,128)S(1)} %get-tuple-element.190), channel_id=1, source_target_pairs={{0,16},{16,32},{32,48},{48,64},{64,80},{80,96},{96,112},{1,17},{17... | collective-permute-start | bytes 245768 | tf_op jit(solution)/shard_map/ppermute | solution.py:33
  303.3 12.5 %collective-permute-start.33 = (f32[2,80,34,1]{1,0,3,2:T(2,128)S(1)}, f32[2,80,34,1]{1,0,3,2:T(2,128)S(1)}, u32[]{:S(2)}, u32[]{:S(2)}) collective-permute-start(f32[2,80,34,1]{1,0,3,2:T(2,128)S(1)} %copy.133), channel_id=1, source_target_pairs={{1,0},{2,1},{3,2},{4,3},{5,4},{6,5},{7,6},{8,7},{9,8},{10,9},{11,1... | collective-permute-start | bytes 65288 | tf_op jit(solution)/shard_map/ppermute | solution.py:35
  307.5 10.8 %collective-permute-start.32 = (f32[2,80,34,1]{1,0,3,2:T(2,128)S(1)}, f32[2,80,34,1]{1,0,3,2:T(2,128)S(1)}, u32[]{:S(2)}, u32[]{:S(2)}) collective-permute-start(f32[2,80,34,1]{1,0,3,2:T(2,128)S(1)} %copy.131), channel_id=1, source_target_pairs={{0,1},{1,2},{2,3},{3,4},{4,5},{5,6},{6,7},{7,8},{8,9},{9,10},{10,1... | collective-permute-start | bytes 65288 | tf_op jit(solution)/shard_map/ppermute | solution.py:33
  331.1 36.2 %all-to-all-start.1 = ((f32[128,1,128]{2,1,0:T(1,128)}), f32[128,1,128]{2,1,0:T(1,128)S(1)}, u32[]{:S(2)}, u32[]{:S(2)}) async-start(f32[128,1,128]{2,1,0:T(1,128)} %bitcast.114), calls=%async_computation.1 | async-start | bytes 131072 | tf_op jit(solution)/shard_map/all_to_all | solution.py:281
  358.1 9.2 %copy-start.53 = (s32[32,128]{1,0:T(8,128)S(1)}, s32[32,128]{1,0:T(8,128)}, u32[]{:S(2)}) copy-start(s32[32,128]{1,0:T(8,128)} %param.31) | copy-start | bytes 49156
  358.1 9.2 %copy-start.55 = (f32[32,128]{1,0:T(8,128)S(1)}, f32[32,128]{1,0:T(8,128)}, u32[]{:S(2)}) copy-start(f32[32,128]{1,0:T(8,128)} %param.32) | copy-start | bytes 49156
  358.2 9.2 %copy-start.59 = (pred[32]{0:T(512)(128)(4,1)S(1)}, pred[32]{0:T(512)(128)(4,1)}, u32[]{:S(2)}) copy-start(pred[32]{0:T(512)(128)(4,1)} %copy-done.58) | copy-start | bytes 100
  358.2 9.2 %copy-start.63 = (s32[32]{0:T(128)S(1)}, s32[32]{0:T(128)}, u32[]{:S(2)}) copy-start(s32[32]{0:T(128)} %copy-done.62) | copy-start | bytes 388
  (38 other events, 151.8 us)
where the time goes:
time: 374 us; the launch traced here: 368 us
  starting transfers between devices  174 us (47%)
  local copies, waits for them, and re-layouts  78.7 us (21%)
  other arithmetic  69.1 us (18%)
  matrix products  28.8 us (8%)
  waiting for transfers between devices  14.9 us (4%)
    ppermute x16, starting transfers between devices, extended(): lax.ppermute(tail, axis, [(i, (i + 1) % count) for i in range(ends)])  93.3 us
    add x4, other arithmetic, ocean_substep(): updated = center + lateral + wet_mid * vertical  33 us
    slice x15, local copies, waits for them, and re-layouts, extended(): lax.slice_in_dim(cells, cells.shape[dim] - width, cells.shape[dim], axis=...  28.6 us
    all_to_all x1, starting transfers between devices, per_device(): lax.all_to_all(outgoing.reshape(size_x * size_y, capacity, col_count), ('...  27.6 us
    all_to_all x1, starting transfers between devices, per_device(): lax.all_to_all(returning.reshape(size_x * size_y, capacity, col_count), (...  27.1 us
    dot_general x3, matrix products, apply_operator(): jnp.einsum('ab,bkij->akij', element_matrix, stacked, precision=lax.Precis...  25.2 us
    ppermute x16, starting transfers between devices, extended(): lax.ppermute(head, axis, [((i + 1) % count, i) for i in range(ends)])  20.8 us
    mul x3, other arithmetic, apply_operator(): products = products * weights_ext[None, :, :row_count + 1, :col_count + 1]  13.1 us
  transfers between devices with their start and end apart: 36, of which 9 were waited for; matrix products, arithmetic and copies ran while one was open for 28% of the time, Pallas kernels for 0%

commit v1 on v0

v1 whole, which is shorter than its diff:
```python
import jax
import jax.numpy as jnp
from jax import lax
from jax.experimental import pallas as pl
from jax.experimental.pallas import tpu as pltpu
from jax.sharding import PartitionSpec as P

MESH = pl.DeviceIdType.MESH
F32 = jnp.float32

LANES = 128
SUB = 8
ROWS = 32
TILES = ROWS // SUB
ZO = 80
NODES = 11
CELLS = 10
STEPS = 4
SWEEPS = 3
CHUNK = 8
FBASE = 8
FSPAN = (ZO + 2) * ROWS
FROWS = 2 * FBASE + 2 * FSPAN
VSPAN = 40
VROWS = (NODES + 16) * VSPAN

relax_weight = 0.6
shift_term = 0.2
vert_mix = 0.1
heat_gamma = 0.5
heat_factor = 0.05
salt_factor = 0.05
salt_ref = 34.5
freeze_slope = -0.0573
freeze_base = 0.0832
freeze_depth = 0.761
melt_factor = 0.2
draft_ratio = 0.89

MASS = {"s": 1.0 / 4.0, "d": 1.0 / 12.0}


def same_weight(z, x, y, along):
    wx, wy = (4.0, 1.0) if along == 0 else (1.0, 4.0)
    total = 0.0
    if x == "d":
        total += wx * MASS[y] * MASS[z]
    if y == "d":
        total += wy * MASS[x] * MASS[z]
    if z == "d":
        total += MASS[x] * MASS[y]
    return total


DIAGONAL = 2.0 / 3.0


def iota(shape, axis):
    return lax.broadcasted_iota(jnp.int32, shape, axis)


def roll(value, shift, axis):
    size = value.shape[axis]
    if isinstance(shift, int):
        shift = shift % size
        if shift == 0:
            return value
    return pltpu.roll(value, shift, axis)


def plane_sums(lo, lo_right, hi, hi_right):
    ls, ld = lo + lo_right, lo_right - lo
    hs, hd = hi + hi_right, hi_right - hi
    return {"ss": ls + hs, "sd": ld + hd, "ds": hs - ls, "dd": hd - ld}


def element_forces(u_low, u_high, v_low, v_high, mu):
    u, v = {}, {}
    for xy in ("ss", "sd", "ds", "dd"):
        if xy != "ss":
            u["s" + xy] = u_low[xy] + u_high[xy]
            v["s" + xy] = v_low[xy] + v_high[xy]
        u["d" + xy] = u_high[xy] - u_low[xy]
        v["d" + xy] = v_high[xy] - v_low[xy]
    scaled = {}

    def times_mu(factor):
        if factor not in scaled:
            scaled[factor] = mu * factor
        return scaled[factor]

    fu, fv = {}, {}
    for key in u:
        z, xy = key[0], key[1:]
        for along, mine, other, out in ((0, u, v, fu), (1, v, u, fv)):
            own = same_weight(z, xy[0], xy[1], along)
            if xy in ("ds", "sd"):
                first = xy == "ds"
                double = first if along == 0 else not first
                cross = MASS[z] * (2.0 if double else 1.0) / 4.0
                swapped = z + ("sd" if first else "ds")
                out[key] = times_mu(own) * (mine[key] + (cross / own) * other[swapped])
            else:
                out[key] = times_mu(own) * mine[key]
    return fu, fv


def lower_part(f):
    out = {xy: f["s" + xy] - f["d" + xy] for xy in ("sd", "ds", "dd")}
    out["ss"] = -f["dss"]
    return out


def upper_part(f):
    out = {xy: f["s" + xy] + f["d" + xy] for xy in ("sd", "ds", "dd")}
    out["ss"] = f["dss"]
    return out


def packed_place(field, chunk):
    return field + (chunk // 8) * (2 - field), (chunk % 8) * 16 + (chunk // 8) * (32 * field)


def kernel(
    force, visc, drag, imask, thick, target, temp, salt, diff, omask, source,
    vel_out, thick_out, temp_out, salt_out,
    fa, fb, coef, opack, orow, rpack, rrow, merged,
    va, vb, mu, rdiag, ipack, imsg, rside, rmsg, rcorner,
    edge_e, col_lo, col_hi, col_mu, col_q, row_q, row_mu,
    wpack, wmsg, rwpack, rwmsg, rwcorner,
    pad_in, draft, tbl, mid, fwd, got,
    in_sem, o_send, o_recv, i_send, i_recv, w_send, w_recv, a_send, a_recv, b_send, b_recv,
):
    gx, gy = lax.axis_index("gx"), lax.axis_index("gy")
    nx, ny = lax.axis_size("gx"), lax.axis_size("gy")

    def at(dx, dy):
        return (lax.rem(gx + (dx + nx), nx), lax.rem(gy + (dy + ny), ny))

    north, south, west, east = at(-1, 0), at(1, 0), at(0, -1), at(0, 1)
    corners = (at(-1, -1), at(-1, 1), at(1, -1), at(1, 1))

    lane8 = iota((SUB, LANES), 1)
    sub8 = iota((SUB, LANES), 0)
    pair8 = lane8 // 2

    loads = []
    for field, ref in ((0, temp), (1, salt)):
        start = FBASE + field * FSPAN + ROWS
        loads.append(pltpu.make_async_copy(ref, fa.at[pl.ds(start, ZO * ROWS)], in_sem.at[field]))
    for copy in loads:
        copy.start()
    barrier = pltpu.get_barrier_semaphore()
    peers = [north, south, *corners]
    peers += [at(0, q) for q in range(1, ny)] + [at(p, 0) for p in range(2, nx - 1)]
    for peer in peers:
        pl.semaphore_signal(barrier, inc=1, device_id=peer, device_id_type=MESH)

    has_n = (gx > 0).astype(F32)
    has_s = (gx < nx - 1).astype(F32)
    has_w = (gy > 0).astype(F32)
    has_e = (gy < ny - 1).astype(F32)

    sends = []

    def send(src, dst, ssem, rsem, device):
        copy = pltpu.make_async_remote_copy(
            src_ref=src, dst_ref=dst, send_sem=ssem, recv_sem=rsem, device_id=device, device_id_type=MESH
        )
        copy.start()
        sends.append(copy)
        return copy

    wet_ice = imask[...].astype(F32)
    wmsg[...] = jnp.zeros_like(wmsg)
    va[...] = jnp.zeros_like(va)
    vb[...] = jnp.zeros_like(vb)
    edge_e[...] = jnp.zeros_like(edge_e)
    col_lo[...] = jnp.zeros_like(col_lo)
    col_hi[...] = jnp.zeros_like(col_hi)
    col_mu[...] = jnp.zeros_like(col_mu)
    for t in range(TILES):
        acc = jnp.zeros((SUB, LANES), F32)
        wet_t = wet_ice[t * SUB : (t + 1) * SUB]
        for k in range(CELLS):
            rows = pl.ds(k * ROWS + t * SUB, SUB)
            weight = visc[rows] * wet_t
            mu[pl.ds(SUB + k * ROWS + t * SUB, SUB)] = weight
            acc = jnp.where(pair8 == k, roll(weight, 2 * k + 1, 1), acc)
        wpack[pl.ds(t * SUB, SUB)] = acc
    wmsg[pl.ds(0, 8)] = mu[pl.ds(SUB + ROWS - 1, 8, stride=ROWS)]
    wmsg[pl.ds(8, 2)] = mu[pl.ds(SUB + 8 * ROWS + ROWS - 1, 2, stride=ROWS)]
    wmsg[pl.ds(16, 1)] = wpack[pl.ds(ROWS - 1, 1)]

    lane1 = iota((SUB, LANES), 1)
    to_row = jnp.full((SUB, LANES), -1, jnp.int32)
    from_row = jnp.full((SUB, LANES), -1, jnp.int32)
    to_col = [jnp.full((SUB, LANES), -1, jnp.int32) for _ in range(TILES)]
    from_col = [jnp.full((SUB, LANES), -1, jnp.int32) for _ in range(TILES)]
    for i in range(ROWS):
        to_row = jnp.where(lane1 == i, target[i], to_row)
        from_row = jnp.where(lane1 == i, source[i], from_row)
        to_col[i // SUB] = jnp.where(sub8 == i % SUB, target[i], to_col[i // SUB])
        from_col[i // SUB] = jnp.where(sub8 == i % SUB, source[i], from_col[i // SUB])

    def slot_of(ids):
        device = ids >> 5
        return jnp.where(ids >= 0, (device & (ny - 1)) * nx + (device >> 4), -1)

    def by_slot(row):
        slots = slot_of(row)
        return jnp.concatenate(
            [(sub8 + n * SUB == slots).astype(F32) for n in range(LANES // SUB)], axis=0
        )

    def by_device(cols):
        return jnp.concatenate(
            [((lane8 == (ids >> 5)) & (ids >= 0)).astype(F32) for ids in cols], axis=0
        )

    def pick(one_hot, values):
        return jnp.dot(one_hot, values, precision=lax.Precision.HIGHEST, preferred_element_type=F32)

    pad_in[...] = jnp.zeros_like(pad_in)
    pad_in[pl.ds(0, ROWS)] = draft_ratio * thick[...]
    tbl[0] = pick(by_slot(to_row), pad_in[...])

    for copy in loads:
        copy.wait()

    def guard(ref):
        for field in range(2):
            base = FBASE + field * FSPAN
            ref[pl.ds(base, ROWS)] = ref[pl.ds(base + ROWS, ROWS)]
            ref[pl.ds(base + (ZO + 1) * ROWS, ROWS)] = ref[pl.ds(base + ZO * ROWS, ROWS)]

    def put_pack(r, field, chunk, t, acc):
        vec, lane = packed_place(field, chunk)
        rows = pl.ds(pl.multiple_of(vec * ROWS + t * SUB, SUB), SUB)
        shifted = pltpu.roll(acc, lane, 1)
        mine = (lane8 >= lane) & (lane8 < lane + 16)
        opack[r, rows] = jnp.where(mine, shifted, opack[r, rows])

    def put_rows(r, ref, field, chunk):
        base = FBASE + field * FSPAN + ROWS + chunk * (CHUNK * ROWS)
        rows = pl.ds(pl.multiple_of(field * ZO + chunk * CHUNK, SUB), SUB)
        orow[r, 0, rows] = ref[pl.ds(base, SUB, stride=ROWS)]
        orow[r, 1, rows] = ref[pl.ds(base + ROWS - 1, SUB, stride=ROWS)]

    opack[...] = jnp.zeros_like(opack)
    orow[...] = jnp.zeros_like(orow)

    def first_edges(chunk, carry):
        for field in range(2):
            base = FBASE + field * FSPAN + ROWS + chunk * (CHUNK * ROWS)
            for t in range(TILES):
                acc = jnp.zeros((SUB, LANES), F32)
                for j in range(CHUNK):
                    value = fa[pl.ds(pl.multiple_of(base + j * ROWS + t * SUB, SUB), SUB)]
                    acc = jnp.where(pair8 == j, roll(value, 2 * j + 1, 1), acc)
                put_pack(0, field, chunk, t, acc)
            put_rows(0, fa, field, chunk)
        return carry

    lax.fori_loop(0, ZO // CHUNK, first_edges, 0)
    guard(fa)
    wet = omask[...].astype(F32)
    diffusion = diff[...]
    orow[0, 0, pl.ds(2 * ZO, 1)] = diffusion[0:1]
    orow[0, 0, pl.ds(2 * ZO + 1, 1)] = wet[0:1]
    orow[0, 1, pl.ds(2 * ZO, 1)] = diffusion[ROWS - 1 :]
    orow[0, 1, pl.ds(2 * ZO + 1, 1)] = wet[ROWS - 1 :]
    for t in range(TILES):
        rows = pl.ds(2 * ROWS + t * SUB, SUB)
        acc = opack[0, rows]
        acc = jnp.where(pair8 == 32, roll(diffusion[t * SUB : (t + 1) * SUB], 65, 1), acc)
        acc = jnp.where(pair8 == 33, roll(wet[t * SUB : (t + 1) * SUB], 67, 1), acc)
        opack[0, rows] = acc

    pl.semaphore_wait(barrier, len(peers))

    def send_ocean(r):
        return [
            send(orow.at[r, 0], rrow.at[r, 1], o_send.at[r, 0], o_recv.at[r, 0], north),
            send(orow.at[r, 1], rrow.at[r, 0], o_send.at[r, 1], o_recv.at[r, 1], south),
            send(opack.at[r], rpack.at[r, 1], o_send.at[r, 2], o_recv.at[r, 2], west),
            send(opack.at[r], rpack.at[r, 0], o_send.at[r, 3], o_recv.at[r, 3], east),
        ]

    def scatter_first(n):
        copies = []
        for q in range(1, ny):
            peer = at(0, q)
            copies.append(
                send(
                    tbl.at[n, pl.ds(pl.multiple_of(peer[1] * nx, nx), nx)],
                    mid.at[n, pl.ds(pl.multiple_of(gy * nx, nx), nx)],
                    a_send.at[n, q], a_recv.at[n, q], peer,
                )
            )
        own = pl.ds(pl.multiple_of(gy * nx, nx), nx)
        mid[n, own] = tbl[n, own]
        return copies

    def scatter_second(n, copies):
        for copy in copies:
            copy.wait_recv()
        for p in range(nx):
            fwd[n, pl.ds(p * ny, ny)] = mid[n, pl.ds(p, ny, stride=nx)]
        copies = []
        for p in range(1, nx):
            peer = at(p, 0)
            copies.append(
                send(
                    fwd.at[n, pl.ds(pl.multiple_of(peer[0] * ny, ny), ny)],
                    got.at[n, pl.ds(pl.multiple_of(gx * ny, ny), ny)],
                    b_send.at[n, p], b_recv.at[n, p], peer,
                )
            )
        own = pl.ds(pl.multiple_of(gx * ny, ny), ny)
        got[n, own] = fwd[n, own]
        return copies

    weights = [
        send(wmsg, rwmsg, w_send.at[0], w_recv.at[0], south),
        send(wpack, rwpack, w_send.at[1], w_recv.at[1], east),
        send(wmsg.at[pl.ds(16, 8)], rwcorner, w_send.at[2], w_recv.at[2], corners[3]),
    ]
    ocean = send_ocean(0)
    coupling = scatter_first(0)

    for copy in weights:
        copy.wait_recv()
    row_mu[...] = rwmsg[pl.ds(0, 16)] * has_n
    even = (lane8 & 1) == 0
    for t in range(TILES):
        col_mu[pl.ds(SUB + t * SUB, SUB)] = jnp.where(even, rwpack[pl.ds(t * SUB, SUB)] * has_w, 0.0)
    even1 = (iota((1, LANES), 1) & 1) == 0
    col_mu[pl.ds(SUB - 1, 1)] = jnp.where(even1, rwcorner[pl.ds(0, 1)] * (has_w * has_n), 0.0)

    def put_ice_edges(r, ref):
        for c in range(2):
            for edge in range(2):
                start = c * NODES * VSPAN + edge * (ROWS - 1)
                imsg[r, edge, pl.ds(c * 16, 16)] = ref[pl.ds(start, 16, stride=VSPAN)]
        imsg[r, 0, pl.ds(32, 1)] = ipack[r, pl.ds(0, 1)]
        imsg[r, 1, pl.ds(32, 1)] = ipack[r, pl.ds(ROWS - 1, 1)]

    def send_ice(r):
        copies = [
            send(imsg.at[r, 0], rmsg.at[r, 1], i_send.at[r, 0], i_recv.at[r, 0], north),
            send(imsg.at[r, 1], rmsg.at[r, 0], i_send.at[r, 1], i_recv.at[r, 1], south),
            send(ipack.at[r], rside.at[r, 1], i_send.at[r, 2], i_recv.at[r, 2], west),
            send(ipack.at[r], rside.at[r, 0], i_send.at[r, 3], i_recv.at[r, 3], east),
        ]
        for n, device in enumerate(corners):
            src = imsg.at[r, n // 2, pl.ds(32, 8)]
            copies.append(send(src, rcorner.at[r, 3 - n], i_send.at[r, 4 + n], i_recv.at[r, 4 + n], device))
        return copies

    imsg[...] = jnp.zeros_like(imsg)
    for t in range(TILES):
        cols = col_mu[pl.ds(SUB + t * SUB, SUB)] + col_mu[pl.ds(SUB - 1 + t * SUB, SUB)]
        cols = cols + roll(cols, 2, 1)
        acc = jnp.zeros((SUB, LANES), F32)
        below = None
        for k in range(NODES):
            layer = None
            if k < CELLS:
                start = SUB + k * ROWS + t * SUB
                up = mu[pl.ds(start - 1, SUB)]
                if t == 0:
                    up = jnp.where(sub8 == 0, row_mu[pl.ds(k, 1)], up)
                layer = mu[pl.ds(start, SUB)] + up
            total = layer if below is None else (below if layer is None else layer + below)
            below = layer
            left = jnp.where(lane8 == 0, roll(cols, -2 * k, 1), roll(total, 1, 1))
            diagonal = DIAGONAL * (total + left) + shift_term
            if k == 0:
                diagonal = diagonal + drag[pl.ds(t * SUB, SUB)]
            factor = relax_weight / diagonal
            rdiag[pl.ds(k * ROWS + t * SUB, SUB)] = factor
            for c in range(2):
                value = force[pl.ds((c * NODES + k) * ROWS + t * SUB, SUB)] * factor
                va[pl.ds((c * NODES + k) * VSPAN + t * SUB, SUB)] = value
                acc = jnp.where(pair8 == 32 * c + k, roll(value, 64 * c + 2 * k + 1, 1), acc)
        ipack[0, pl.ds(t * SUB, SUB)] = acc
    put_ice_edges(0, va)
    ice = send_ice(0)

    def take_ocean(r, copies):
        for copy in copies:
            copy.wait_recv()
        for n in range(3 * TILES):
            rows = pl.ds(n * SUB, SUB)
            from_e = roll(rpack[r, 1, rows], -1, 1)
            from_w = roll(rpack[r, 0, rows], 1, 1)
            merged[rows] = jnp.where(even, from_e, from_w)

    take_ocean(0, ocean)
    for t in range(TILES):
        rows = slice(t * SUB, (t + 1) * SUB)
        d, w = diffusion[rows], wet[rows]

        def around(mine, plane, n):
            whole = plane
            up = roll(mine, 1, 0)
            above = rrow[0, 0, pl.ds(2 * ZO + n, 1)] if t == 0 else whole[t * SUB - 1 : t * SUB]
            up = jnp.where(sub8 == 0, above, up)
            down = roll(mine, -1, 0)
            below = rrow[0, 1, pl.ds(2 * ZO + n, 1)] if t == TILES - 1 else whole[(t + 1) * SUB : (t + 1) * SUB + 1]
            down = jnp.where(sub8 == SUB - 1, below, down)
            edge = roll(merged[pl.ds(2 * ROWS + t * SUB, SUB)], 127 - 64 - 2 * n, 1)
            left = jnp.where(lane8 == 0, edge, roll(mine, 1, 1))
            right = jnp.where(lane8 == LANES - 1, edge, roll(mine, -1, 1))
            return up, down, left, right

        near_d = around(d, diffusion, 0)
        up_w, down_w, left_w, right_w = around(w, wet, 1)
        if t == 0:
            up_w = jnp.where(sub8 == 0, up_w * has_n, up_w)
        if t == TILES - 1:
            down_w = jnp.where(sub8 == SUB - 1, down_w * has_s, down_w)
        left_w = jnp.where(lane8 == 0, left_w * has_w, left_w)
        right_w = jnp.where(lane8 == LANES - 1, right_w * has_e, right_w)
        total = 2.0 * vert_mix * w
        for n, (near, near_w) in enumerate(zip(near_d, (up_w, down_w, left_w, right_w))):
            face = 0.5 * (d + near) * w * near_w
            coef[pl.ds((n + 1) * ROWS + t * SUB, SUB)] = face
            total = total + face
        coef[pl.ds(t * SUB, SUB)] = 1.0 - total
        coef[pl.ds(5 * ROWS + t * SUB, SUB)] = vert_mix * w

    def melt_of(temp_top, salt_top, t):
        freezing = freeze_slope * (salt_ref + salt_top) + freeze_base - freeze_depth * draft[pl.ds(t * SUB, SUB)]
        return heat_gamma * (temp_top - freezing) * (10.0 * coef[pl.ds(5 * ROWS + t * SUB, SUB)])

    def ocean_chunk(s, chunk, src, dst, top):
        for t in range(TILES):
            cs = [coef[pl.ds(n * ROWS + t * SUB, SUB)] for n in range(6)]
            first = []
            for field in range(2):
                base = FBASE + field * FSPAN + ROWS + chunk * (CHUNK * ROWS) + t * SUB
                if not isinstance(base, int):
                    base = pl.multiple_of(base, SUB)
                vec, lane = packed_place(field, chunk)
                packed = merged[pl.ds(pl.multiple_of(vec * ROWS + t * SUB, SUB), SUB)]
                packed = pltpu.roll(packed, lax.rem(LANES - lane, LANES), 1)
                acc = jnp.zeros((SUB, LANES), F32)
                prev = src[pl.ds(base - ROWS, SUB)]
                cur = src[pl.ds(base, SUB)]
                news = []
                for j in range(CHUNK):
                    row = base + j * ROWS
                    nxt = src[pl.ds(row + ROWS, SUB)]
                    up = src[pl.ds(row - 1, SUB)]
                    down = src[pl.ds(row + 1, SUB)]
                    level = field * ZO + chunk * CHUNK + j
                    if t == 0:
                        up = jnp.where(sub8 == 0, rrow[s, 0, pl.ds(level, 1)], up)
                    if t == TILES - 1:
                        down = jnp.where(sub8 == SUB - 1, rrow[s, 1, pl.ds(level, 1)], down)
                    edge = roll(packed, 127 - 2 * j, 1)
                    left = jnp.where(lane8 == 0, edge, roll(cur, 1, 1))
                    right = jnp.where(lane8 == LANES - 1, edge, roll(cur, -1, 1))
                    new = (
                        cs[0] * cur
                        + (cs[1] * up + cs[2] * down)
                        + (cs[3] * left + cs[4] * right)
                        + cs[5] * (prev + nxt)
                    )
                    news.append(new)
                    prev, cur = cur, nxt
                first.append(news)
            if top:
                temp_top, salt_top = first[0][0], first[1][0]
                rate = melt_of(temp_top, salt_top, t)
                first[0][0] = temp_top - heat_factor * rate
                first[1][0] = salt_top - salt_factor * rate * (salt_ref + salt_top) / salt_ref
            for field in range(2):
                acc = jnp.zeros((SUB, LANES), F32)
                for j in range(CHUNK):
                    new = first[field][j]
                    if s < STEPS - 1:
                        row = FBASE + field * FSPAN + ROWS + chunk * (CHUNK * ROWS) + t * SUB + j * ROWS
                        if not isinstance(row, int):
                            row = pl.multiple_of(row, SUB)
                        dst[pl.ds(row, SUB)] = new
                        acc = jnp.where(pair8 == j, roll(new, 2 * j + 1, 1), acc)
                    else:
                        row = chunk * (CHUNK * ROWS) + j * ROWS + t * SUB
                        if not isinstance(row, int):
                            row = pl.multiple_of(row, SUB)
                        dst[field][pl.ds(row, SUB)] = new
                if s < STEPS - 1:
                    put_pack(s + 1, field, chunk, t, acc)
        if s < STEPS - 1:
            for field in range(2):
                put_rows(s + 1, dst, field, chunk)

    def ocean_rest(s, src, dst):
        def body(chunk, carry):
            ocean_chunk(s, chunk, src, dst, False)
            return carry

        lax.fori_loop(1, ZO // CHUNK, body, 0)

    def ice_sweep(r, copies, src, dst):
        last = r == SWEEPS - 1
        for copy in copies:
            copy.wait_recv()
        for c in range(2):
            for k in range(NODES):
                src[pl.ds((c * NODES + k) * VSPAN + ROWS, 1)] = rmsg[r, 1, pl.ds(c * 16 + k, 1)] * has_s
        for t in range(TILES):
            rows = pl.ds(t * SUB, SUB)
            edge_e[rows] = rside[r, 1, rows] * has_e
            col_lo[pl.ds(SUB + t * SUB, SUB)] = rside[r, 0, rows] * has_w
            col_hi[pl.ds(SUB + t * SUB, SUB)] = roll(ipack[r, rows], -1, 1)
        edge_e[pl.ds(ROWS, 1)] = rcorner[r, 3, pl.ds(0, 1)] * (has_e * has_s)
        col_lo[pl.ds(SUB - 1, 1)] = rcorner[r, 0, pl.ds(0, 1)] * (has_w * has_n)
        col_lo[pl.ds(SUB + ROWS, 1)] = rcorner[r, 2, pl.ds(0, 1)] * (has_w * has_s)
        col_hi[pl.ds(SUB - 1, 1)] = roll(rmsg[r, 0, pl.ds(32, 1)] * has_n, -1, 1)
        col_hi[pl.ds(SUB + ROWS, 1)] = roll(rmsg[r, 1, pl.ds(32, 1)] * has_s, -1, 1)
        for t in range(TILES + 1):
            start = SUB - 1 + t * SUB
            if t == TILES:
                start = ROWS
            lo0, lo1 = col_lo[pl.ds(start, SUB)], col_lo[pl.ds(start + 1, SUB)]
            hi0, hi1 = col_hi[pl.ds(start, SUB)], col_hi[pl.ds(start + 1, SUB)]
            planes = []
            for c in range(2):
                parts = [roll(value, 64 * c, 1) for value in (lo0, hi0, lo1, hi1)]
                low = plane_sums(*parts)
                planes += [low, {key: roll(value, -2, 1) for key, value in low.items()}]
            fu, fv = element_forces(*planes, col_mu[pl.ds(start, SUB)])
            for c, f in enumerate((fu, fv)):
                low, high = lower_part(f), upper_part(f)
                node = {key: low[key] + roll(high[key], 2, 1) for key in low}
                col_q[2 * c, pl.ds(start - SUB + 1, SUB)] = node["ss"] + node["sd"]
                col_q[2 * c + 1, pl.ds(start - SUB + 1, SUB)] = node["ds"] + node["dd"]
        lane16, sub16 = iota((16, LANES), 1), iota((16, LANES), 0)

        def upright(row, offset):
            chosen = jnp.where(lane16 == 2 * sub16 + offset, row, 0.0)
            return jnp.sum(chosen, axis=1, keepdims=True)

        planes = []
        for c in range(2):
            lo = rmsg[r, 0, pl.ds(c * 16, 16)]
            hi = imsg[r, 0, pl.ds(c * 16, 16)]
            lo_end = upright(rcorner[r, 1, pl.ds(0, 1)] * (has_e * has_n), 64 * c + 1)
            hi_end = upright(edge_e[pl.ds(0, 1)], 64 * c + 1)
            lo_right = jnp.where(lane16 == LANES - 1, lo_end, roll(lo, -1, 1))
            hi_right = jnp.where(lane16 == LANES - 1, hi_end, roll(hi, -1, 1))
            low = plane_sums(lo, lo_right, hi, hi_right)
            planes += [low, {key: roll(value, -1, 0) for key, value in low.items()}]
        fu, fv = element_forces(*planes, row_mu[...])
        for c, f in enumerate((fu, fv)):
            low, high = lower_part(f), upper_part(f)
            node = {key: low[key] + roll(high[key], 1, 0) for key in low}
            ends = []
            for n, x in enumerate("sd"):
                behind = upright(col_q[2 * c + n, pl.ds(0, 1)], 0)
                shifted = roll(node[x + "s"] + node[x + "d"], 1, 1)
                ends.append(node[x + "s"] - node[x + "d"] + jnp.where(lane16 == 0, behind, shifted))
            row_q[pl.ds(c * 16, 16)] = ends[0] + ends[1]
        pass_down = [[None] * NODES, [None] * NODES]
        for t in range(TILES):
            here, next_row = edge_e[pl.ds(t * SUB, SUB)], edge_e[pl.ds(t * SUB + 1, SUB)]
            strips = [[col_q[2 * c + n, pl.ds(1 + t * SUB, SUB)] for n in range(2)] for c in range(2)]
            acc = jnp.zeros((SUB, LANES), F32)
            below, carried = None, None
            for k in range(NODES + 1):
                planes = None
                if k < NODES:
                    planes = []
                    for c in range(2):
                        start = (c * NODES + k) * VSPAN + t * SUB
                        lo, hi = src[pl.ds(start, SUB)], src[pl.ds(start + 1, SUB)]
                        shift = 127 - (64 * c + 2 * k + 1)
                        lo_right = jnp.where(lane8 == LANES - 1, roll(here, shift, 1), roll(lo, -1, 1))
                        hi_right = jnp.where(lane8 == LANES - 1, roll(next_row, shift, 1), roll(hi, -1, 1))
                        planes.append(plane_sums(lo, lo_right, hi, hi_right))
                if k >= 1:
                    level = k - 1
                    nodes, ups = [None, None], [None, None]
                    if level < CELLS:
                        weight = mu[pl.ds(SUB + level * ROWS + t * SUB, SUB)]
                        forces = element_forces(below[0], planes[0], below[1], planes[1], weight)
                        for c in range(2):
                            nodes[c], ups[c] = lower_part(forces[c]), upper_part(forces[c])
                            if carried is not None:
                                nodes[c] = {key: nodes[c][key] + carried[c][key] for key in nodes[c]}
                    else:
                        nodes = carried
                    carried = ups
                    factor = rdiag[pl.ds(level * ROWS + t * SUB, SUB)]
                    for c in range(2):
                        node = nodes[c]
                        shift = -(2 * level)
                        sides = []
                        for n, x in enumerate("sd"):
                            before = jnp.where(
                                lane8 == 0,
                                roll(strips[c][n], shift, 1),
                                roll(node[x + "s"] + node[x + "d"], 1, 1),
                            )
                            sides.append(node[x + "s"] - node[x + "d"] + before)
                        down = roll(sides[0] + sides[1], 1, 0)
                        over = row_q[pl.ds(c * 16 + level, 1)] if t == 0 else pass_down[c][level]
                        pass_down[c][level] = down[0:1]
                        applied = sides[0] - sides[1] + jnp.where(sub8 == 0, over, down)
                        value = src[pl.ds((c * NODES + level) * VSPAN + t * SUB, SUB)]
                        extra = shift_term
                        if level == 0:
                            extra = shift_term + drag[pl.ds(t * SUB, SUB)]
                        applied = applied + extra * value
                        row = (c * NODES + level) * ROWS + t * SUB
                        value = value + (force[pl.ds(row, SUB)] - applied) * factor
                        if last:
                            dst[pl.ds(row, SUB)] = value
                        else:
                            dst[pl.ds((c * NODES + level) * VSPAN + t * SUB, SUB)] = value
                            place = 64 * c + 2 * level + 1
                            acc = jnp.where(pair8 == 32 * c + level, roll(value, place, 1), acc)
                below = planes
            if not last:
                ipack[r + 1, pl.ds(t * SUB, SUB)] = acc
        if last:
            return None
        put_ice_edges(r + 1, dst)
        return send_ice(r + 1)

    coupling = scatter_second(0, coupling)
    ocean_rest(0, fa, fb)
    for copy in coupling:
        copy.wait_recv()
    draft[...] = pick(by_device(from_col), got[0])
    ocean_chunk(0, 0, fa, fb, True)
    guard(fb)
    ocean = send_ocean(1)
    ice = ice_sweep(0, ice, va, vb)

    take_ocean(1, ocean)
    ocean_chunk(1, 0, fb, fa, True)
    ocean_rest(1, fb, fa)
    guard(fa)
    ocean = send_ocean(2)
    ice = ice_sweep(1, ice, vb, va)

    take_ocean(2, ocean)
    ocean_chunk(2, 0, fa, fb, True)
    ocean_rest(2, fa, fb)
    guard(fb)
    ocean = send_ocean(3)
    take_ocean(3, ocean)
    ocean_chunk(3, 0, fb, (temp_out, salt_out), True)
    for t in range(TILES):
        rows = pl.ds(t * SUB, SUB)
        pad_in[rows] = melt_of(temp_out[rows], salt_out[rows], t)
    tbl[1] = pick(by_slot(from_row), pad_in[...])
    coupling = scatter_first(1)
    ice_sweep(2, ice, va, vel_out)
    coupling = scatter_second(1, coupling)
    ocean_rest(3, fb, (temp_out, salt_out))
    for copy in coupling:
        copy.wait_recv()
    melt = pick(by_device(to_col), got[1])
    thick_out[...] = thick[...] - melt_factor * melt * wet_ice
    for copy in sends:
        copy.wait_send()


def per_device(
    ice_force, ice_visc, ice_drag, ice_mask, ice_thick, ice_target,
    ocean_temp, ocean_salt, ocean_diff, ocean_mask, ocean_source,
):
    def flat(array):
        return array.reshape(-1, LANES)

    vmem = pl.BlockSpec(memory_space=pltpu.VMEM)
    smem = pl.BlockSpec(memory_space=pltpu.SMEM)
    hbm = pl.BlockSpec(memory_space=pl.ANY)
    dma = pltpu.SemaphoreType.DMA

    def buf(*shape):
        return pltpu.VMEM((*shape, LANES), F32)

    nx, ny = lax.axis_size("gx"), lax.axis_size("gy")
    scratch = [
        buf(FROWS), buf(FROWS), buf(6 * ROWS), buf(STEPS, 3 * ROWS), buf(STEPS, 2, 2 * ZO + SUB),
        buf(STEPS, 2, 3 * ROWS), buf(STEPS, 2, 2 * ZO + SUB), buf(3 * ROWS),
        buf(VROWS), buf(VROWS), buf(2 * SUB + CELLS * ROWS), buf(NODES * ROWS),
        buf(SWEEPS, ROWS), buf(SWEEPS, 2, 40), buf(SWEEPS, 2, ROWS), buf(SWEEPS, 2, 40), buf(SWEEPS, 4, SUB),
        buf(ROWS + SUB), buf(ROWS + 2 * SUB), buf(ROWS + 2 * SUB), buf(ROWS + 2 * SUB),
        buf(4, ROWS + SUB), buf(32), buf(16),
        buf(ROWS), buf(24), buf(ROWS), buf(24), buf(SUB),
        buf(LANES), buf(ROWS), buf(2, LANES), buf(2, LANES), buf(2, LANES), buf(2, LANES),
        dma((2,)), dma((STEPS, 4)), dma((STEPS, 4)), dma((SWEEPS, 8)), dma((SWEEPS, 8)),
        dma((3,)), dma((3,)), dma((2, ny)), dma((2, ny)), dma((2, nx)), dma((2, nx)),
    ]
    velocity, thickness, temp, salt = pl.pallas_call(
        kernel,
        out_shape=[
            jax.ShapeDtypeStruct((2 * NODES * ROWS, LANES), F32),
            jax.ShapeDtypeStruct((ROWS, LANES), F32),
            jax.ShapeDtypeStruct((ZO * ROWS, LANES), F32),
            jax.ShapeDtypeStruct((ZO * ROWS, LANES), F32),
        ],
        in_specs=[vmem, vmem, vmem, vmem, vmem, smem, hbm, hbm, vmem, vmem, smem],
        out_specs=[vmem] * 4,
        scratch_shapes=scratch,
        compiler_params=pltpu.CompilerParams(
            collective_id=0, has_side_effects=True, vmem_limit_bytes=40 * 1024 * 1024
        ),
    )(
        flat(ice_force), flat(ice_visc), ice_drag, ice_mask, ice_thick, ice_target,
        flat(ocean_temp), flat(ocean_salt), ocean_diff, ocean_mask, ocean_source,
    )
    return (
        velocity.reshape(ice_force.shape),
        thickness,
        temp.reshape(ocean_temp.shape),
        salt.reshape(ocean_salt.shape),
    )


def solution(mesh):
    in_specs = (
        P(None, None, "gx", "gy"),
        P(None, "gx", "gy"),
        P("gx", "gy"),
        P("gx", "gy"),
        P("gx", "gy"),
        P(("gx", "gy")),
        P(None, "gx", "gy"),
        P(None, "gx", "gy"),
        P("gx", "gy"),
        P("gx", "gy"),
        P(("gx", "gy")),
    )
    out_specs = (P(None, None, "gx", "gy"), P("gx", "gy"), P(None, "gx", "gy"), P(None, "gx", "gy"))
    return jax.shard_map(per_device, mesh=mesh, in_specs=in_specs, out_specs=out_specs, check_vma=False)
```

time: 374 us -> 83.2 us (0.22); the launches traced: 368 us -> 81.7 us
  starting transfers between devices: 174 us -> 0 us
  other arithmetic: 69.1 us -> 0 us
  Pallas kernels: 0 us -> 68.2 us
  local copies, waits for them, and re-layouts: 78.7 us -> 12.9 us
  matrix products: 28.8 us -> 0 us
  waiting for transfers between devices: 14.9 us -> 0 us
    ppermute x34 -> x0, starting transfers between devices: 119 us -> none  [the longest x16 93.3 us: extended(): lax.ppermute(tail, axis, [(i, (i + 1) % count) for i in range(ends)])]
    pallas_call x0 -> x1, Pallas kernels: none -> 68.2 us  [per_device(): pl.pallas_call(kernel, out_shape=[jax.ShapeDtypeStruct((2 * NODES * ROWS,...]
    all_to_all x2 -> x0, starting transfers between devices: 54.7 us -> none  [the longest x1 27.6 us: per_device(): lax.all_to_all(outgoing.reshape(size_x * size_y, capacity, col_count), ('...]
    slice x23 -> x0, local copies, waits for them, and re-layouts: 40.8 us -> none  [the longest x15 28.6 us: extended(): lax.slice_in_dim(cells, cells.shape[dim] - width, cells.shape[dim], axis=...]
    add x10 -> x0, other arithmetic: 34.9 us -> none  [the longest x4 33 us: ocean_substep(): updated = center + lateral + wet_mid * vertical]
    dot_general x7 -> x0, matrix products: 28.8 us -> none  [the longest x3 25.2 us: apply_operator(): jnp.einsum('ab,bkij->akij', element_matrix, stacked, precision=lax.Precis...]
    mul x16 -> x0, other arithmetic: 23.3 us -> none  [the longest x3 13.1 us: apply_operator(): products = products * weights_ext[None, :, :row_count + 1, :col_count + 1]]
    ppermute x8 -> x0, local copies, waits for them, and re-layouts: 22.6 us -> none  [the longest x4 11.4 us: extended(): lax.ppermute(head, axis, [((i + 1) % count, i) for i in range(ends)])]
  transfers between devices with their start and end apart: 36 -> 0, of which waited for: 9 -> 0; matrix products, arithmetic and copies ran while one was open for 28% -> 0% of each run, Pallas kernels for 0% -> 0%
where the time goes in v1:
time: 83.2 us; the launch traced here: 81.7 us
  Pallas kernels  68.2 us (82%)
  local copies, waits for them, and re-layouts  12.9 us (16%)
    pallas_call x1, Pallas kernels, per_device(): pl.pallas_call(kernel, out_shape=[jax.ShapeDtypeStruct((2 * NODES * ROWS,...  68.2 us
    unnamed x26, local copies, waits for them, and re-layouts  12.9 us

profile of v1, /device:TPU:0, one launch (start us, length us, event | category | flops | bytes accessed | tf_op | source)
XLA Modules:
  0.0 81.7 jit_solution(5787288783881111892)
XLA Ops:
  0.6 0.0 copy-start
  0.6 1.3 %copy-done = f32[80,32,128]{2,1,0:T(8,128)S(1)} copy-done((f32[80,32,128]{2,1,0:T(8,128)S(1)}, f32[80,32,128]{2,1,0:T(8,128)}, u32[]{:S(2)}) %copy-start) | copy-done | bytes 1310744
  2.0 0.0 copy-start.1
  2.0 1.3 %copy-done.1 = f32[80,32,128]{2,1,0:T(8,128)S(1)} copy-done((f32[80,32,128]{2,1,0:T(8,128)S(1)}, f32[80,32,128]{2,1,0:T(8,128)}, u32[]{:S(2)}) %copy-start.1) | copy-done | bytes 1310744
  3.3 0.0 copy-start.2
  3.3 1.0 %copy-done.2 = f32[2,11,32,128]{3,2,1,0:T(8,128)S(1)} copy-done((f32[2,11,32,128]{3,2,1,0:T(8,128)S(1)}, f32[2,11,32,128]{3,2,1,0:T(8,128)}, u32[]{:S(2)}) %copy-start.2) | copy-done | bytes 360472
  4.3 0.0 copy-start.3
  4.3 0.9 %copy-done.3 = f32[10,32,128]{2,1,0:T(8,128)S(1)} copy-done((f32[10,32,128]{2,1,0:T(8,128)S(1)}, f32[10,32,128]{2,1,0:T(8,128)}, u32[]{:S(2)}) %copy-start.3) | copy-done | bytes 163864
  5.2 0.0 copy-start.4
  5.2 0.7 copy-done.4
  5.9 0.0 copy-start.5
  5.9 0.7 copy-done.5
  6.6 0.0 copy-start.6
  6.6 0.7 copy-done.6
  7.3 0.0 copy-start.7
  7.3 0.7 copy-done.7
  8.0 0.0 copy-start.8
  8.0 0.7 copy-done.8
  8.8 0.0 copy-start.9
  8.8 0.7 copy-done.9
  9.4 0.0 copy-start.10
  9.4 0.7 copy-done.10
  10.1 68.2 %shard_map.138 = (f32[704,128]{1,0:T(8,128)S(1)}, f32[32,128]{1,0:T(8,128)S(1)}, f32[2560,128]{1,0:T(8,128)S(1)}, f32[2560,128]{1,0:T(8,128)S(1)}) custom-call(f32[704,128]{1,0:T(8,128)S(1)} %bitcast.11, f32[320,128]{1,0:T(8,128)S(1)} %bitcast.13, f32[32,128]{1,0:T(8,128)S(1)} %copy-done.4, s32[32,128]{1,0:T(8,128)S(1)} %copy-done.5, ...), custom_call_target="tpu_custom_call" | custom-call | tf_op jit(solution)/shard_map/pallas_call | solution.py:703
  78.2 0.7 copy.19
  79.0 0.6 copy.20
  79.6 1.1 %copy.21 = f32[80,32,128]{2,1,0:T(8,128)} copy(f32[80,32,128]{2,1,0:T(8,128)S(1)} %bitcast.10) | data formatting | bytes 2621440
  80.6 1.1 %copy.22 = f32[80,32,128]{2,1,0:T(8,128)} copy(f32[80,32,128]{2,1,0:T(8,128)S(1)} %bitcast.9) | data formatting | bytes 2621440
Async XLA Ops:
  0.6 1.3 %copy-start = (f32[80,32,128]{2,1,0:T(8,128)S(1)}, f32[80,32,128]{2,1,0:T(8,128)}, u32[]{:S(2)}) copy-start(f32[80,32,128]{2,1,0:T(8,128)} %param.17) | copy-start | bytes 3932164
  2.0 1.3 %copy-start.1 = (f32[80,32,128]{2,1,0:T(8,128)S(1)}, f32[80,32,128]{2,1,0:T(8,128)}, u32[]{:S(2)}) copy-start(f32[80,32,128]{2,1,0:T(8,128)} %param.18) | copy-start | bytes 3932164
  3.3 1.0 %copy-start.2 = (f32[2,11,32,128]{3,2,1,0:T(8,128)S(1)}, f32[2,11,32,128]{3,2,1,0:T(8,128)}, u32[]{:S(2)}) copy-start(f32[2,11,32,128]{3,2,1,0:T(8,128)} %param.11) | copy-start | bytes 1081348
  4.3 0.9 %copy-start.3 = (f32[10,32,128]{2,1,0:T(8,128)S(1)}, f32[10,32,128]{2,1,0:T(8,128)}, u32[]{:S(2)}) copy-start(f32[10,32,128]{2,1,0:T(8,128)} %param.12) | copy-start | bytes 491524
  5.2 0.7 copy-start.4
  5.9 0.7 copy-start.5
  6.6 0.7 copy-start.6
  7.3 0.7 copy-start.7
  8.0 0.7 copy-start.8
  8.8 0.7 copy-start.9
  9.4 0.7 copy-start.10

commit v2 on v1

--- a/solution.py
+++ b/solution.py
@@ -122,10 +122,12 @@
 
 
 def kernel(
-    force, visc, drag, imask, thick, target, temp, salt, diff, omask, source,
+    force_in, visc_in, drag_in, imask_in, thick_in, target_in, temp_in, salt_in, diff_in, omask_in, source_in,
     vel_out, thick_out, temp_out, salt_out,
+    force, visc, drag, imask, thick, target, diff, omask, source,
     fa, fb, coef, opack, orow, rpack, rrow, merged,
     va, vb, mu, rdiag, ipack, imsg, rside, rmsg, rcorner,
+    vright, low_y, high_y, shifts, sides,
     edge_e, col_lo, col_hi, col_mu, col_q, row_q, row_mu,
     wpack, wmsg, rwpack, rwmsg, rwcorner,
     pad_in, draft, tbl, mid, fwd, got,
@@ -144,10 +146,12 @@
     sub8 = iota((SUB, LANES), 0)
     pair8 = lane8 // 2
 
-    loads = []
-    for field, ref in ((0, temp), (1, salt)):
+    pairs = [(visc_in, visc), (imask_in, imask), (thick_in, thick), (target_in, target), (source_in, source)]
+    for field, ref in ((0, temp_in), (1, salt_in)):
         start = FBASE + field * FSPAN + ROWS
-        loads.append(pltpu.make_async_copy(ref, fa.at[pl.ds(start, ZO * ROWS)], in_sem.at[field]))
+        pairs.append((ref, fa.at[pl.ds(start, ZO * ROWS)]))
+    pairs += [(diff_in, diff), (omask_in, omask), (drag_in, drag), (force_in, force)]
+    loads = [pltpu.make_async_copy(src, dst, in_sem.at[n]) for n, (src, dst) in enumerate(pairs)]
     for copy in loads:
         copy.start()
     barrier = pltpu.get_barrier_semaphore()
@@ -171,7 +175,6 @@
         sends.append(copy)
         return copy
 
-    wet_ice = imask[...].astype(F32)
     wmsg[...] = jnp.zeros_like(wmsg)
     va[...] = jnp.zeros_like(va)
     vb[...] = jnp.zeros_like(vb)
@@ -179,6 +182,17 @@
     col_lo[...] = jnp.zeros_like(col_lo)
     col_hi[...] = jnp.zeros_like(col_hi)
     col_mu[...] = jnp.zeros_like(col_mu)
+    imsg[...] = jnp.zeros_like(imsg)
+    pad_in[...] = jnp.zeros_like(pad_in)
+    opack[...] = jnp.zeros_like(opack)
+    orow[...] = jnp.zeros_like(orow)
+    row_no, col_no = iota((2 * LANES, 2 * LANES), 0) % LANES, iota((2 * LANES, 2 * LANES), 1)
+    before = (row_no == col_no - 1) & (col_no < LANES)
+    after = (row_no == col_no + 1 - LANES) & (col_no >= LANES)
+    shifts[...] = (before | after).astype(F32).astype(jnp.bfloat16)
+    for copy in loads[:5]:
+        copy.wait()
+    wet_ice = imask[...].astype(F32)
     for t in range(TILES):
         acc = jnp.zeros((SUB, LANES), F32)
         wet_t = wet_ice[t * SUB : (t + 1) * SUB]
@@ -221,11 +235,10 @@
     def pick(one_hot, values):
         return jnp.dot(one_hot, values, precision=lax.Precision.HIGHEST, preferred_element_type=F32)
 
-    pad_in[...] = jnp.zeros_like(pad_in)
     pad_in[pl.ds(0, ROWS)] = draft_ratio * thick[...]
     tbl[0] = pick(by_slot(to_row), pad_in[...])
 
-    for copy in loads:
+    for copy in loads[5:]:
         copy.wait()
 
     def guard(ref):
@@ -246,9 +259,6 @@
         rows = pl.ds(pl.multiple_of(field * ZO + chunk * CHUNK, SUB), SUB)
         orow[r, 0, rows] = ref[pl.ds(base, SUB, stride=ROWS)]
         orow[r, 1, rows] = ref[pl.ds(base + ROWS - 1, SUB, stride=ROWS)]
-
-    opack[...] = jnp.zeros_like(opack)
-    orow[...] = jnp.zeros_like(orow)
 
     def first_edges(chunk, carry):
         for field in range(2):
@@ -358,7 +368,6 @@
             copies.append(send(src, rcorner.at[r, 3 - n], i_send.at[r, 4 + n], i_recv.at[r, 4 + n], device))
         return copies
 
-    imsg[...] = jnp.zeros_like(imsg)
     for t in range(TILES):
         cols = col_mu[pl.ds(SUB + t * SUB, SUB)] + col_mu[pl.ds(SUB - 1 + t * SUB, SUB)]
         cols = cols + roll(cols, 2, 1)
@@ -436,6 +445,17 @@
         return heat_gamma * (temp_top - freezing) * (10.0 * coef[pl.ds(5 * ROWS + t * SUB, SUB)])
 
     def ocean_chunk(s, chunk, src, dst, top):
+        for field in range(2):
+            base = FBASE + field * FSPAN + ROWS + chunk * (CHUNK * ROWS)
+            if not isinstance(base, int):
+                base = pl.multiple_of(base, SUB)
+            values = src[pl.ds(base, CHUNK * ROWS)]
+            high = values.astype(jnp.bfloat16)
+            rest = (values - high.astype(F32)).astype(jnp.bfloat16)
+            both = jnp.concatenate([high, rest], axis=1)
+            sides[pl.ds(field * CHUNK * ROWS, CHUNK * ROWS)] = jnp.dot(
+                both, shifts[...], preferred_element_type=F32
+            )
         for t in range(TILES):
             cs = [coef[pl.ds(n * ROWS + t * SUB, SUB)] for n in range(6)]
             first = []
@@ -461,8 +481,9 @@
                     if t == TILES - 1:
                         down = jnp.where(sub8 == SUB - 1, rrow[s, 1, pl.ds(level, 1)], down)
                     edge = roll(packed, 127 - 2 * j, 1)
-                    left = jnp.where(lane8 == 0, edge, roll(cur, 1, 1))
-                    right = jnp.where(lane8 == LANES - 1, edge, roll(cur, -1, 1))
+                    beside = pl.ds(field * CHUNK * ROWS + j * ROWS + t * SUB, SUB)
+                    left = jnp.where(lane8 == 0, edge, sides[beside, :LANES])
+                    right = jnp.where(lane8 == LANES - 1, edge, sides[beside, LANES:])
                     new = (
                         cs[0] * cur
                         + (cs[1] * up + cs[2] * down)
@@ -537,8 +558,9 @@
             for c, f in enumerate((fu, fv)):
                 low, high = lower_part(f), upper_part(f)
                 node = {key: low[key] + roll(high[key], 2, 1) for key in low}
-                col_q[2 * c, pl.ds(start - SUB + 1, SUB)] = node["ss"] + node["sd"]
-                col_q[2 * c + 1, pl.ds(start - SUB + 1, SUB)] = node["ds"] + node["dd"]
+                behind = {x: node[x + "s"] + node[x + "d"] for x in "sd"}
+                col_q[2 * c, pl.ds(start - SUB + 1, SUB)] = behind["s"] - behind["d"]
+                col_q[2 * c + 1, pl.ds(start - SUB + 1, SUB)] = behind["s"] + behind["d"]
         lane16, sub16 = iota((16, LANES), 1), iota((16, LANES), 0)
 
         def upright(row, offset):
@@ -559,17 +581,18 @@
         for c, f in enumerate((fu, fv)):
             low, high = lower_part(f), upper_part(f)
             node = {key: low[key] + roll(high[key], 1, 0) for key in low}
-            ends = []
-            for n, x in enumerate("sd"):
-                behind = upright(col_q[2 * c + n, pl.ds(0, 1)], 0)
-                shifted = roll(node[x + "s"] + node[x + "d"], 1, 1)
-                ends.append(node[x + "s"] - node[x + "d"] + jnp.where(lane16 == 0, behind, shifted))
-            row_q[pl.ds(c * 16, 16)] = ends[0] + ends[1]
-        pass_down = [[None] * NODES, [None] * NODES]
+            for n, sign in enumerate((-1.0, 1.0)):
+                parts = [node[x + "s"] + sign * node[x + "d"] for x in "sd"]
+                row_q[pl.ds((2 * n + c) * 16, 16)] = parts[0] + parts[1]
+        for c in range(2):
+            for k in range(NODES):
+                shift = 127 - (64 * c + 2 * k + 1)
+                for t in range(TILES + 1):
+                    rows = pl.ds((c * NODES + k) * VSPAN + t * SUB, SUB)
+                    edge = roll(edge_e[pl.ds(t * SUB, SUB)], shift, 1)
+                    vright[rows] = jnp.where(lane8 == LANES - 1, edge, roll(src[rows], -1, 1))
+        pass_down = {}
         for t in range(TILES):
-            here, next_row = edge_e[pl.ds(t * SUB, SUB)], edge_e[pl.ds(t * SUB + 1, SUB)]
-            strips = [[col_q[2 * c + n, pl.ds(1 + t * SUB, SUB)] for n in range(2)] for c in range(2)]
-            acc = jnp.zeros((SUB, LANES), F32)
             below, carried = None, None
             for k in range(NODES + 1):
                 planes = None
@@ -577,11 +600,8 @@
                     planes = []
                     for c in range(2):
                         start = (c * NODES + k) * VSPAN + t * SUB
-                        lo, hi = src[pl.ds(start, SUB)], src[pl.ds(start + 1, SUB)]
-                        shift = 127 - (64 * c + 2 * k + 1)
-                        lo_right = jnp.where(lane8 == LANES - 1, roll(here, shift, 1), roll(lo, -1, 1))
-                        hi_right = jnp.where(lane8 == LANES - 1, roll(next_row, shift, 1), roll(hi, -1, 1))
-                        planes.append(plane_sums(lo, lo_right, hi, hi_right))
+                        lo, hi = pl.ds(start, SUB), pl.ds(start + 1, SUB)
+                        planes.append(plane_sums(src[lo], vright[lo], src[hi], vright[hi]))
                 if k >= 1:
                     level = k - 1
                     nodes, ups = [None, None], [None, None]
@@ -595,40 +615,45 @@
                     else:
                         nodes = carried
                     carried = ups
-                    factor = rdiag[pl.ds(level * ROWS + t * SUB, SUB)]
                     for c in range(2):
                         node = nodes[c]
-                        shift = -(2 * level)
-                        sides = []
-                        for n, x in enumerate("sd"):
-                            before = jnp.where(
-                                lane8 == 0,
-                                roll(strips[c][n], shift, 1),
-                                roll(node[x + "s"] + node[x + "d"], 1, 1),
-                            )
-                            sides.append(node[x + "s"] - node[x + "d"] + before)
-                        down = roll(sides[0] + sides[1], 1, 0)
-                        over = row_q[pl.ds(c * 16 + level, 1)] if t == 0 else pass_down[c][level]
-                        pass_down[c][level] = down[0:1]
-                        applied = sides[0] - sides[1] + jnp.where(sub8 == 0, over, down)
-                        value = src[pl.ds((c * NODES + level) * VSPAN + t * SUB, SUB)]
-                        extra = shift_term
-                        if level == 0:
-                            extra = shift_term + drag[pl.ds(t * SUB, SUB)]
-                        applied = applied + extra * value
-                        row = (c * NODES + level) * ROWS + t * SUB
-                        value = value + (force[pl.ds(row, SUB)] - applied) * factor
-                        if last:
-                            dst[pl.ds(row, SUB)] = value
-                        else:
-                            dst[pl.ds((c * NODES + level) * VSPAN + t * SUB, SUB)] = value
-                            place = 64 * c + 2 * level + 1
-                            acc = jnp.where(pair8 == 32 * c + level, roll(value, place, 1), acc)
+                        row = pl.ds((c * NODES + level) * ROWS + t * SUB, SUB)
+                        for n, (sign, place) in enumerate(((-1.0, low_y), (1.0, high_y))):
+                            parts = [node[x + "s"] + sign * node[x + "d"] for x in "sd"]
+                            down = roll(parts[0] + parts[1], 1, 0)
+                            if t == 0:
+                                over = row_q[pl.ds((2 * n + c) * 16 + level, 1)]
+                            else:
+                                over = pass_down[n, c, level]
+                            pass_down[n, c, level] = down[0:1]
+                            place[row] = parts[0] - parts[1] + jnp.where(sub8 == 0, over, down)
                 below = planes
-            if not last:
-                ipack[r + 1, pl.ds(t * SUB, SUB)] = acc
+        for c in range(2):
+            for t in range(TILES):
+                strip = col_q[2 * c, pl.ds(1 + t * SUB, SUB)] + col_q[2 * c + 1, pl.ds(t * SUB, SUB)]
+                for level in range(NODES):
+                    at_row = (c * NODES + level) * ROWS + t * SUB
+                    row = pl.ds(at_row, SUB)
+                    before = jnp.where(lane8 == 0, roll(strip, -2 * level, 1), roll(high_y[row], 1, 1))
+                    value = src[pl.ds((c * NODES + level) * VSPAN + t * SUB, SUB)]
+                    extra = shift_term
+                    if level == 0:
+                        extra = shift_term + drag[pl.ds(t * SUB, SUB)]
+                    applied = low_y[row] + before + extra * value
+                    value = value + (force[row] - applied) * rdiag[pl.ds(level * ROWS + t * SUB, SUB)]
+                    if last:
+                        dst[row] = value
+                    else:
+                        dst[pl.ds((c * NODES + level) * VSPAN + t * SUB, SUB)] = value
         if last:
             return None
+        for t in range(TILES):
+            acc = jnp.zeros((SUB, LANES), F32)
+            for c in range(2):
+                for level in range(NODES):
+                    value = dst[pl.ds((c * NODES + level) * VSPAN + t * SUB, SUB)]
+                    acc = jnp.where(pair8 == 32 * c + level, roll(value, 64 * c + 2 * level + 1, 1), acc)
+            ipack[r + 1, pl.ds(t * SUB, SUB)] = acc
         put_ice_edges(r + 1, dst)
         return send_ice(r + 1)
 
@@ -677,27 +702,34 @@
     ocean_temp, ocean_salt, ocean_diff, ocean_mask, ocean_source,
 ):
     def flat(array):
-        return array.reshape(-1, LANES)
+        return pltpu.with_memory_space_constraint(array.reshape(-1, LANES), pltpu.HBM)
+
+    def held(array):
+        return pltpu.with_memory_space_constraint(array, pltpu.HBM)
 
     vmem = pl.BlockSpec(memory_space=pltpu.VMEM)
-    smem = pl.BlockSpec(memory_space=pltpu.SMEM)
-    hbm = pl.BlockSpec(memory_space=pl.ANY)
+    hbm = pl.BlockSpec(memory_space=pltpu.HBM)
     dma = pltpu.SemaphoreType.DMA
 
     def buf(*shape):
         return pltpu.VMEM((*shape, LANES), F32)
 
     nx, ny = lax.axis_size("gx"), lax.axis_size("gy")
+    whole = pltpu.VMEM((ROWS, LANES), jnp.int32)
+    ids = pltpu.SMEM((ROWS,), jnp.int32)
     scratch = [
+        buf(2 * NODES * ROWS), buf(CELLS * ROWS), buf(ROWS), whole, buf(ROWS), ids, buf(ROWS), whole, ids,
         buf(FROWS), buf(FROWS), buf(6 * ROWS), buf(STEPS, 3 * ROWS), buf(STEPS, 2, 2 * ZO + SUB),
         buf(STEPS, 2, 3 * ROWS), buf(STEPS, 2, 2 * ZO + SUB), buf(3 * ROWS),
         buf(VROWS), buf(VROWS), buf(2 * SUB + CELLS * ROWS), buf(NODES * ROWS),
         buf(SWEEPS, ROWS), buf(SWEEPS, 2, 40), buf(SWEEPS, 2, ROWS), buf(SWEEPS, 2, 40), buf(SWEEPS, 4, SUB),
+        buf(VROWS), buf(2 * NODES * ROWS), buf(2 * NODES * ROWS),
+        pltpu.VMEM((2 * LANES, 2 * LANES), jnp.bfloat16), pltpu.VMEM((2 * CHUNK * ROWS, 2 * LANES), F32),
         buf(ROWS + SUB), buf(ROWS + 2 * SUB), buf(ROWS + 2 * SUB), buf(ROWS + 2 * SUB),
-        buf(4, ROWS + SUB), buf(32), buf(16),
+        buf(4, ROWS + SUB), buf(64), buf(16),
         buf(ROWS), buf(24), buf(ROWS), buf(24), buf(SUB),
         buf(LANES), buf(ROWS), buf(2, LANES), buf(2, LANES), buf(2, LANES), buf(2, LANES),
-        dma((2,)), dma((STEPS, 4)), dma((STEPS, 4)), dma((SWEEPS, 8)), dma((SWEEPS, 8)),
+        dma((11,)), dma((STEPS, 4)), dma((STEPS, 4)), dma((SWEEPS, 8)), dma((SWEEPS, 8)),
         dma((3,)), dma((3,)), dma((2, ny)), dma((2, ny)), dma((2, nx)), dma((2, nx)),
     ]
     velocity, thickness, temp, salt = pl.pallas_call(
@@ -708,15 +740,15 @@
             jax.ShapeDtypeStruct((ZO * ROWS, LANES), F32),
             jax.ShapeDtypeStruct((ZO * ROWS, LANES), F32),
         ],
-        in_specs=[vmem, vmem, vmem, vmem, vmem, smem, hbm, hbm, vmem, vmem, smem],
+        in_specs=[hbm] * 11,
         out_specs=[vmem] * 4,
         scratch_shapes=scratch,
         compiler_params=pltpu.CompilerParams(
             collective_id=0, has_side_effects=True, vmem_limit_bytes=40 * 1024 * 1024
         ),
     )(
-        flat(ice_force), flat(ice_visc), ice_drag, ice_mask, ice_thick, ice_target,
-        flat(ocean_temp), flat(ocean_salt), ocean_diff, ocean_mask, ocean_source,
+        flat(ice_force), flat(ice_visc), held(ice_drag), held(ice_mask), held(ice_thick), held(ice_target),
+        flat(ocean_temp), flat(ocean_salt), held(ocean_diff), held(ocean_mask), held(ocean_source),
     )
     return (
         velocity.reshape(ice_force.shape),

time: 83.2 us -> 63.4 us (0.76); the launches traced: 81.7 us -> 63.1 us
  local copies, waits for them, and re-layouts: 12.9 us -> 3.45 us
  Pallas kernels: 68.2 us -> 59 us
    unnamed x26 -> x4, local copies, waits for them, and re-layouts: 12.9 us -> 3.45 us
    pallas_call x1, Pallas kernels: 68.2 us -> 59 us  [per_device(): pl.pallas_call(kernel, out_shape=[jax.ShapeDtypeStruct((2 * NODES * ROWS,...]
where the time goes in v2:
time: 63.4 us; the launch traced here: 63.1 us
  Pallas kernels  59 us (93%)
  local copies, waits for them, and re-layouts  3.45 us (5%)
  between operations  0.64 us (1%)
    pallas_call x1, Pallas kernels, per_device(): pl.pallas_call(kernel, out_shape=[jax.ShapeDtypeStruct((2 * NODES * ROWS,...  59 us
    unnamed x4, local copies, waits for them, and re-layouts  3.45 us

profile of v2, /device:TPU:0, one launch (start us, length us, event | category | flops | bytes accessed | tf_op | source)
XLA Modules:
  0.0 63.1 jit_solution(15053249271568395962)
XLA Ops:
  0.6 59.0 %shard_map.138 = (f32[704,128]{1,0:T(8,128)S(1)}, f32[32,128]{1,0:T(8,128)S(1)}, f32[2560,128]{1,0:T(8,128)S(1)}, f32[2560,128]{1,0:T(8,128)S(1)}) custom-call(f32[704,128]{1,0:T(8,128)} %bitcast.12, f32[320,128]{1,0:T(8,128)} %bitcast.13, f32[32,128]{1,0:T(8,128)} %drag_in.1, s32[32,128]{1,0:T(8,128)} %imask_in.1, f32[32,128]{1,0:T(8,128)} %thick_in.1, ...), custom_call_target="tpu_custom_call" | custom-call | tf_op jit(solution)/shard_map/pallas_call | solution.py:735
  59.6 0.7 %copy.19 = f32[2,11,32,128]{3,2,1,0:T(8,128)} copy(f32[2,11,32,128]{3,2,1,0:T(8,128)S(1)} %bitcast.9) | data formatting | bytes 720896
  60.4 0.6 copy.20
  61.0 1.1 %copy.21 = f32[80,32,128]{2,1,0:T(8,128)} copy(f32[80,32,128]{2,1,0:T(8,128)S(1)} %bitcast.8) | data formatting | bytes 2621440
  62.0 1.1 %copy.22 = f32[80,32,128]{2,1,0:T(8,128)} copy(f32[80,32,128]{2,1,0:T(8,128)S(1)} %bitcast.7) | data formatting | bytes 2621440

commit v3 on v2

--- a/solution.py
+++ b/solution.py
@@ -117,8 +117,26 @@
     return out
 
 
-def packed_place(field, chunk):
-    return field + (chunk // 8) * (2 - field), (chunk % 8) * 16 + (chunk // 8) * (32 * field)
+GROUPS = {
+    "top": ((0, 1), (128, 32), (144, 24), (144, 8)),
+    "mid": ((1, 5), (0, 64), (0, 64), (0, 32)),
+    "low": ((5, 10), (64, 64), (64, 80), (64, 40)),
+}
+ORDER = ("top", "mid", "low")
+PACK_ROWS = 160
+STATIC_ROW = 160
+
+
+def packed_place(group, field, chunk):
+    first = GROUPS[group][0][0]
+    if group == "top":
+        return 4 * ROWS, 16 * field
+    return (field + (2 if group == "low" else 0)) * ROWS, (chunk - first) * 16
+
+
+def level_row(group, field, chunk):
+    start, span = GROUPS[group][3]
+    return start + field * span + (chunk - GROUPS[group][0][0]) * CHUNK
 
 
 def kernel(
@@ -238,64 +256,7 @@
     pad_in[pl.ds(0, ROWS)] = draft_ratio * thick[...]
     tbl[0] = pick(by_slot(to_row), pad_in[...])
 
-    for copy in loads[5:]:
-        copy.wait()
-
-    def guard(ref):
-        for field in range(2):
-            base = FBASE + field * FSPAN
-            ref[pl.ds(base, ROWS)] = ref[pl.ds(base + ROWS, ROWS)]
-            ref[pl.ds(base + (ZO + 1) * ROWS, ROWS)] = ref[pl.ds(base + ZO * ROWS, ROWS)]
-
-    def put_pack(r, field, chunk, t, acc):
-        vec, lane = packed_place(field, chunk)
-        rows = pl.ds(pl.multiple_of(vec * ROWS + t * SUB, SUB), SUB)
-        shifted = pltpu.roll(acc, lane, 1)
-        mine = (lane8 >= lane) & (lane8 < lane + 16)
-        opack[r, rows] = jnp.where(mine, shifted, opack[r, rows])
-
-    def put_rows(r, ref, field, chunk):
-        base = FBASE + field * FSPAN + ROWS + chunk * (CHUNK * ROWS)
-        rows = pl.ds(pl.multiple_of(field * ZO + chunk * CHUNK, SUB), SUB)
-        orow[r, 0, rows] = ref[pl.ds(base, SUB, stride=ROWS)]
-        orow[r, 1, rows] = ref[pl.ds(base + ROWS - 1, SUB, stride=ROWS)]
-
-    def first_edges(chunk, carry):
-        for field in range(2):
-            base = FBASE + field * FSPAN + ROWS + chunk * (CHUNK * ROWS)
-            for t in range(TILES):
-                acc = jnp.zeros((SUB, LANES), F32)
-                for j in range(CHUNK):
-                    value = fa[pl.ds(pl.multiple_of(base + j * ROWS + t * SUB, SUB), SUB)]
-                    acc = jnp.where(pair8 == j, roll(value, 2 * j + 1, 1), acc)
-                put_pack(0, field, chunk, t, acc)
-            put_rows(0, fa, field, chunk)
-        return carry
-
-    lax.fori_loop(0, ZO // CHUNK, first_edges, 0)
-    guard(fa)
-    wet = omask[...].astype(F32)
-    diffusion = diff[...]
-    orow[0, 0, pl.ds(2 * ZO, 1)] = diffusion[0:1]
-    orow[0, 0, pl.ds(2 * ZO + 1, 1)] = wet[0:1]
-    orow[0, 1, pl.ds(2 * ZO, 1)] = diffusion[ROWS - 1 :]
-    orow[0, 1, pl.ds(2 * ZO + 1, 1)] = wet[ROWS - 1 :]
-    for t in range(TILES):
-        rows = pl.ds(2 * ROWS + t * SUB, SUB)
-        acc = opack[0, rows]
-        acc = jnp.where(pair8 == 32, roll(diffusion[t * SUB : (t + 1) * SUB], 65, 1), acc)
-        acc = jnp.where(pair8 == 33, roll(wet[t * SUB : (t + 1) * SUB], 67, 1), acc)
-        opack[0, rows] = acc
-
     pl.semaphore_wait(barrier, len(peers))
-
-    def send_ocean(r):
-        return [
-            send(orow.at[r, 0], rrow.at[r, 1], o_send.at[r, 0], o_recv.at[r, 0], north),
-            send(orow.at[r, 1], rrow.at[r, 0], o_send.at[r, 1], o_recv.at[r, 1], south),
-            send(opack.at[r], rpack.at[r, 1], o_send.at[r, 2], o_recv.at[r, 2], west),
-            send(opack.at[r], rpack.at[r, 0], o_send.at[r, 3], o_recv.at[r, 3], east),
-        ]
 
     def scatter_first(n):
         copies = []
@@ -336,8 +297,83 @@
         send(wpack, rwpack, w_send.at[1], w_recv.at[1], east),
         send(wmsg.at[pl.ds(16, 8)], rwcorner, w_send.at[2], w_recv.at[2], corners[3]),
     ]
-    ocean = send_ocean(0)
     coupling = scatter_first(0)
+
+    for copy in loads[5:]:
+        copy.wait()
+
+    def guard(ref, ends):
+        for field in range(2):
+            base = FBASE + field * FSPAN
+            if "top" in ends:
+                ref[pl.ds(base, ROWS)] = ref[pl.ds(base + ROWS, ROWS)]
+            if "low" in ends:
+                ref[pl.ds(base + (ZO + 1) * ROWS, ROWS)] = ref[pl.ds(base + ZO * ROWS, ROWS)]
+
+    def put_pack(r, group, field, chunk, t, acc):
+        first, lane = packed_place(group, field, chunk)
+        rows = pl.ds(first + t * SUB, SUB)
+        shifted = roll(acc, lane, 1)
+        mine = (lane8 >= lane) & (lane8 < lane + 16)
+        opack[r, rows] = jnp.where(mine, shifted, opack[r, rows])
+
+    def put_rows(r, ref, group, field, chunk):
+        base = FBASE + field * FSPAN + ROWS + chunk * (CHUNK * ROWS)
+        start = level_row(group, field, chunk)
+        rows = pl.ds(start if isinstance(start, int) else pl.multiple_of(start, SUB), SUB)
+        orow[r, 0, rows] = ref[pl.ds(base, SUB, stride=ROWS)]
+        orow[r, 1, rows] = ref[pl.ds(base + ROWS - 1, SUB, stride=ROWS)]
+
+    def first_edges(group, chunk):
+        for field in range(2):
+            base = FBASE + field * FSPAN + ROWS + chunk * (CHUNK * ROWS)
+            if not isinstance(base, int):
+                base = pl.multiple_of(base, SUB)
+            for t in range(TILES):
+                acc = jnp.zeros((SUB, LANES), F32)
+                for j in range(CHUNK):
+                    value = fa[pl.ds(base + j * ROWS + t * SUB, SUB)]
+                    acc = jnp.where(pair8 == j, roll(value, 2 * j + 1, 1), acc)
+                put_pack(0, group, field, chunk, t, acc)
+            put_rows(0, fa, group, field, chunk)
+
+    def over_chunks(group, step):
+        def body(chunk, carry):
+            step(group, chunk)
+            return carry
+
+        if group == "top":
+            step(group, 0)
+        else:
+            lax.fori_loop(*GROUPS[group][0], body, 0)
+
+    def send_ocean(r, group):
+        n = ORDER.index(group)
+        cols, rows = (pl.ds(*GROUPS[group][m]) for m in (1, 2))
+        return [
+            send(orow.at[r, 0, rows], rrow.at[r, 1, rows], o_send.at[r, n, 0], o_recv.at[r, n, 0], north),
+            send(orow.at[r, 1, rows], rrow.at[r, 0, rows], o_send.at[r, n, 1], o_recv.at[r, n, 1], south),
+            send(opack.at[r, cols], rpack.at[r, 1, cols], o_send.at[r, n, 2], o_recv.at[r, n, 2], west),
+            send(opack.at[r, cols], rpack.at[r, 0, cols], o_send.at[r, n, 3], o_recv.at[r, n, 3], east),
+        ]
+
+    ocean = {}
+    guard(fa, ("top", "low"))
+    wet = omask[...].astype(F32)
+    diffusion = diff[...]
+    orow[0, 0, pl.ds(STATIC_ROW, 1)] = diffusion[0:1]
+    orow[0, 0, pl.ds(STATIC_ROW + 1, 1)] = wet[0:1]
+    orow[0, 1, pl.ds(STATIC_ROW, 1)] = diffusion[ROWS - 1 :]
+    orow[0, 1, pl.ds(STATIC_ROW + 1, 1)] = wet[ROWS - 1 :]
+    for t in range(TILES):
+        rows = pl.ds(4 * ROWS + t * SUB, SUB)
+        acc = opack[0, rows]
+        acc = jnp.where(pair8 == 32, roll(diffusion[t * SUB : (t + 1) * SUB], 65, 1), acc)
+        acc = jnp.where(pair8 == 33, roll(wet[t * SUB : (t + 1) * SUB], 67, 1), acc)
+        opack[0, rows] = acc
+    for group in ("low", "top", "mid"):
+        over_chunks(group, first_edges)
+        ocean[group] = send_ocean(0, group)
 
     for copy in weights:
         copy.wait_recv()
@@ -397,16 +433,18 @@
     put_ice_edges(0, va)
     ice = send_ice(0)
 
-    def take_ocean(r, copies):
-        for copy in copies:
+    def take_ocean(r, group):
+        for copy in ocean[group]:
             copy.wait_recv()
-        for n in range(3 * TILES):
-            rows = pl.ds(n * SUB, SUB)
+        first, count = GROUPS[group][1]
+        for n in range(count // SUB):
+            rows = pl.ds(first + n * SUB, SUB)
             from_e = roll(rpack[r, 1, rows], -1, 1)
             from_w = roll(rpack[r, 0, rows], 1, 1)
             merged[rows] = jnp.where(even, from_e, from_w)
 
-    take_ocean(0, ocean)
+    coupling = scatter_second(0, coupling)
+    take_ocean(0, "top")
     for t in range(TILES):
         rows = slice(t * SUB, (t + 1) * SUB)
         d, w = diffusion[rows], wet[rows]
@@ -414,12 +452,12 @@
         def around(mine, plane, n):
             whole = plane
             up = roll(mine, 1, 0)
-            above = rrow[0, 0, pl.ds(2 * ZO + n, 1)] if t == 0 else whole[t * SUB - 1 : t * SUB]
+            above = rrow[0, 0, pl.ds(STATIC_ROW + n, 1)] if t == 0 else whole[t * SUB - 1 : t * SUB]
             up = jnp.where(sub8 == 0, above, up)
             down = roll(mine, -1, 0)
-            below = rrow[0, 1, pl.ds(2 * ZO + n, 1)] if t == TILES - 1 else whole[(t + 1) * SUB : (t + 1) * SUB + 1]
+            below = rrow[0, 1, pl.ds(STATIC_ROW + n, 1)] if t == TILES - 1 else whole[(t + 1) * SUB : (t + 1) * SUB + 1]
             down = jnp.where(sub8 == SUB - 1, below, down)
-            edge = roll(merged[pl.ds(2 * ROWS + t * SUB, SUB)], 127 - 64 - 2 * n, 1)
+            edge = roll(merged[pl.ds(4 * ROWS + t * SUB, SUB)], 127 - 64 - 2 * n, 1)
             left = jnp.where(lane8 == 0, edge, roll(mine, 1, 1))
             right = jnp.where(lane8 == LANES - 1, edge, roll(mine, -1, 1))
             return up, down, left, right
@@ -444,7 +482,7 @@
         freezing = freeze_slope * (salt_ref + salt_top) + freeze_base - freeze_depth * draft[pl.ds(t * SUB, SUB)]
         return heat_gamma * (temp_top - freezing) * (10.0 * coef[pl.ds(5 * ROWS + t * SUB, SUB)])
 
-    def ocean_chunk(s, chunk, src, dst, top):
+    def ocean_chunk(s, group, chunk, src, dst):
         for field in range(2):
             base = FBASE + field * FSPAN + ROWS + chunk * (CHUNK * ROWS)
             if not isinstance(base, int):
@@ -463,9 +501,9 @@
                 base = FBASE + field * FSPAN + ROWS + chunk * (CHUNK * ROWS) + t * SUB
                 if not isinstance(base, int):
                     base = pl.multiple_of(base, SUB)
-                vec, lane = packed_place(field, chunk)
-                packed = merged[pl.ds(pl.multiple_of(vec * ROWS + t * SUB, SUB), SUB)]
-                packed = pltpu.roll(packed, lax.rem(LANES - lane, LANES), 1)
+                vec, lane = packed_place(group, field, chunk)
+                packed = merged[pl.ds(vec + t * SUB, SUB)]
+                packed = roll(packed, -lane if isinstance(lane, int) else lax.rem(LANES - lane, LANES), 1)
                 acc = jnp.zeros((SUB, LANES), F32)
                 prev = src[pl.ds(base - ROWS, SUB)]
                 cur = src[pl.ds(base, SUB)]
@@ -475,7 +513,7 @@
                     nxt = src[pl.ds(row + ROWS, SUB)]
                     up = src[pl.ds(row - 1, SUB)]
                     down = src[pl.ds(row + 1, SUB)]
-                    level = field * ZO + chunk * CHUNK + j
+                    level = level_row(group, field, chunk) + j
                     if t == 0:
                         up = jnp.where(sub8 == 0, rrow[s, 0, pl.ds(level, 1)], up)
                     if t == TILES - 1:
@@ -493,7 +531,7 @@
                     news.append(new)
                     prev, cur = cur, nxt
                 first.append(news)
-            if top:
+            if group == "top":
                 temp_top, salt_top = first[0][0], first[1][0]
                 rate = melt_of(temp_top, salt_top, t)
                 first[0][0] = temp_top - heat_factor * rate
@@ -514,17 +552,18 @@
                             row = pl.multiple_of(row, SUB)
                         dst[field][pl.ds(row, SUB)] = new
                 if s < STEPS - 1:
-                    put_pack(s + 1, field, chunk, t, acc)
+                    put_pack(s + 1, group, field, chunk, t, acc)
         if s < STEPS - 1:
             for field in range(2):
-                put_rows(s + 1, dst, field, chunk)
-
-    def ocean_rest(s, src, dst):
-        def body(chunk, carry):
-            ocean_chunk(s, chunk, src, dst, False)
-            return carry
-
-        lax.fori_loop(1, ZO // CHUNK, body, 0)
+                put_rows(s + 1, dst, group, field, chunk)
+
+    def ocean_part(s, group, src, dst, taken=False):
+        if not taken:
+            take_ocean(s, group)
+        over_chunks(group, lambda part, chunk: ocean_chunk(s, part, chunk, src, dst))
+        if s < STEPS - 1:
+            guard(dst, (group,))
+            ocean[group] = send_ocean(s + 1, group)
 
     def ice_sweep(r, copies, src, dst):
         last = r == SWEEPS - 1
@@ -657,38 +696,30 @@
         put_ice_edges(r + 1, dst)
         return send_ice(r + 1)
 
-    coupling = scatter_second(0, coupling)
-    ocean_rest(0, fa, fb)
+    ocean_part(0, "low", fa, fb)
+    ocean_part(0, "mid", fa, fb)
     for copy in coupling:
         copy.wait_recv()
     draft[...] = pick(by_device(from_col), got[0])
-    ocean_chunk(0, 0, fa, fb, True)
-    guard(fb)
-    ocean = send_ocean(1)
+    ocean_part(0, "top", fa, fb, True)
     ice = ice_sweep(0, ice, va, vb)
-
-    take_ocean(1, ocean)
-    ocean_chunk(1, 0, fb, fa, True)
-    ocean_rest(1, fb, fa)
-    guard(fa)
-    ocean = send_ocean(2)
+    ocean_part(1, "low", fb, fa)
+    ocean_part(1, "top", fb, fa)
+    ocean_part(1, "mid", fb, fa)
     ice = ice_sweep(1, ice, vb, va)
-
-    take_ocean(2, ocean)
-    ocean_chunk(2, 0, fa, fb, True)
-    ocean_rest(2, fa, fb)
-    guard(fb)
-    ocean = send_ocean(3)
-    take_ocean(3, ocean)
-    ocean_chunk(3, 0, fb, (temp_out, salt_out), True)
+    ocean_part(2, "top", fa, fb)
+    ocean_part(2, "low", fa, fb)
+    ocean_part(2, "mid", fa, fb)
+    ocean_part(3, "top", fb, (temp_out, salt_out))
     for t in range(TILES):
         rows = pl.ds(t * SUB, SUB)
         pad_in[rows] = melt_of(temp_out[rows], salt_out[rows], t)
     tbl[1] = pick(by_slot(from_row), pad_in[...])
     coupling = scatter_first(1)
     ice_sweep(2, ice, va, vel_out)
+    ocean_part(3, "mid", fb, (temp_out, salt_out))
     coupling = scatter_second(1, coupling)
-    ocean_rest(3, fb, (temp_out, salt_out))
+    ocean_part(3, "low", fb, (temp_out, salt_out))
     for copy in coupling:
         copy.wait_recv()
     melt = pick(by_device(to_col), got[1])
@@ -719,8 +750,8 @@
     ids = pltpu.SMEM((ROWS,), jnp.int32)
     scratch = [
         buf(2 * NODES * ROWS), buf(CELLS * ROWS), buf(ROWS), whole, buf(ROWS), ids, buf(ROWS), whole, ids,
-        buf(FROWS), buf(FROWS), buf(6 * ROWS), buf(STEPS, 3 * ROWS), buf(STEPS, 2, 2 * ZO + SUB),
-        buf(STEPS, 2, 3 * ROWS), buf(STEPS, 2, 2 * ZO + SUB), buf(3 * ROWS),
+        buf(FROWS), buf(FROWS), buf(6 * ROWS), buf(STEPS, PACK_ROWS), buf(STEPS, 2, 2 * ZO + SUB),
+        buf(STEPS, 2, PACK_ROWS), buf(STEPS, 2, 2 * ZO + SUB), buf(PACK_ROWS),
         buf(VROWS), buf(VROWS), buf(2 * SUB + CELLS * ROWS), buf(NODES * ROWS),
         buf(SWEEPS, ROWS), buf(SWEEPS, 2, 40), buf(SWEEPS, 2, ROWS), buf(SWEEPS, 2, 40), buf(SWEEPS, 4, SUB),
         buf(VROWS), buf(2 * NODES * ROWS), buf(2 * NODES * ROWS),
@@ -729,7 +760,7 @@
         buf(4, ROWS + SUB), buf(64), buf(16),
         buf(ROWS), buf(24), buf(ROWS), buf(24), buf(SUB),
         buf(LANES), buf(ROWS), buf(2, LANES), buf(2, LANES), buf(2, LANES), buf(2, LANES),
-        dma((11,)), dma((STEPS, 4)), dma((STEPS, 4)), dma((SWEEPS, 8)), dma((SWEEPS, 8)),
+        dma((11,)), dma((STEPS, 3, 4)), dma((STEPS, 3, 4)), dma((SWEEPS, 8)), dma((SWEEPS, 8)),
         dma((3,)), dma((3,)), dma((2, ny)), dma((2, ny)), dma((2, nx)), dma((2, nx)),
     ]
     velocity, thickness, temp, salt = pl.pallas_call(

time: 63.4 us -> 51.8 us (0.82)
  Pallas kernels: 59 us -> 47.6 us
    pallas_call x1, Pallas kernels: 59 us -> 47.6 us  [per_device(): pl.pallas_call(kernel, out_shape=[jax.ShapeDtypeStruct((2 * NODES * ROWS,...]
where the time goes in v3:
time: 51.8 us; the launch traced here: 51.7 us
  Pallas kernels  47.6 us (92%)
  local copies, waits for them, and re-layouts  3.45 us (7%)
  between operations  0.64 us (1%)
    pallas_call x1, Pallas kernels, per_device(): pl.pallas_call(kernel, out_shape=[jax.ShapeDtypeStruct((2 * NODES * ROWS,...  47.6 us
    unnamed x4, local copies, waits for them, and re-layouts  3.45 us

profile of v3, /device:TPU:0, one launch (start us, length us, event | category | flops | bytes accessed | tf_op | source)
XLA Modules:
  0.0 51.7 jit_solution(16190310599693961597)
XLA Ops:
  0.6 47.6 %shard_map.138 = (f32[704,128]{1,0:T(8,128)S(1)}, f32[32,128]{1,0:T(8,128)S(1)}, f32[2560,128]{1,0:T(8,128)S(1)}, f32[2560,128]{1,0:T(8,128)S(1)}) custom-call(f32[704,128]{1,0:T(8,128)} %bitcast.12, f32[320,128]{1,0:T(8,128)} %bitcast.13, f32[32,128]{1,0:T(8,128)} %drag_in.1, s32[32,128]{1,0:T(8,128)} %imask_in.1, f32[32,128]{1,0:T(8,128)} %thick_in.1, ...), custom_call_target="tpu_custom_call" | custom-call | tf_op jit(solution)/shard_map/pallas_call | solution.py:766
  48.2 0.7 %copy.19 = f32[2,11,32,128]{3,2,1,0:T(8,128)} copy(f32[2,11,32,128]{3,2,1,0:T(8,128)S(1)} %bitcast.9) | data formatting | bytes 720896
  49.0 0.6 %copy.20 = f32[32,128]{1,0:T(8,128)} copy(f32[32,128]{1,0:T(8,128)S(1)} %get-tuple-element.17) | data formatting | bytes 32768
  49.6 1.1 %copy.21 = f32[80,32,128]{2,1,0:T(8,128)} copy(f32[80,32,128]{2,1,0:T(8,128)S(1)} %bitcast.8) | data formatting | bytes 2621440
  50.6 1.1 %copy.22 = f32[80,32,128]{2,1,0:T(8,128)} copy(f32[80,32,128]{2,1,0:T(8,128)S(1)} %bitcast.7) | data formatting | bytes 2621440

commit v4 on v3

--- a/solution.py
+++ b/solution.py
@@ -717,15 +717,24 @@
     tbl[1] = pick(by_slot(from_row), pad_in[...])
     coupling = scatter_first(1)
     ice_sweep(2, ice, va, vel_out)
+    ocean_part(3, "low", fb, (temp_out, salt_out))
+    coupling = scatter_second(1, coupling)
     ocean_part(3, "mid", fb, (temp_out, salt_out))
-    coupling = scatter_second(1, coupling)
-    ocean_part(3, "low", fb, (temp_out, salt_out))
     for copy in coupling:
         copy.wait_recv()
     melt = pick(by_device(to_col), got[1])
     thick_out[...] = thick[...] - melt_factor * melt * wet_ice
     for copy in sends:
         copy.wait_send()
+
+
+def write_out(*refs):
+    srcs, dsts, sem = refs[:4], refs[4:8], refs[8]
+    copies = [pltpu.make_async_copy(src, dst, sem.at[n]) for n, (src, dst) in enumerate(zip(srcs, dsts))]
+    for copy in copies:
+        copy.start()
+    for copy in copies:
+        copy.wait()
 
 
 def per_device(
@@ -763,14 +772,15 @@
         dma((11,)), dma((STEPS, 3, 4)), dma((STEPS, 3, 4)), dma((SWEEPS, 8)), dma((SWEEPS, 8)),
         dma((3,)), dma((3,)), dma((2, ny)), dma((2, ny)), dma((2, nx)), dma((2, nx)),
     ]
-    velocity, thickness, temp, salt = pl.pallas_call(
+    shapes = [
+        jax.ShapeDtypeStruct((2 * NODES * ROWS, LANES), F32),
+        jax.ShapeDtypeStruct((ROWS, LANES), F32),
+        jax.ShapeDtypeStruct((ZO * ROWS, LANES), F32),
+        jax.ShapeDtypeStruct((ZO * ROWS, LANES), F32),
+    ]
+    results = pl.pallas_call(
         kernel,
-        out_shape=[
-            jax.ShapeDtypeStruct((2 * NODES * ROWS, LANES), F32),
-            jax.ShapeDtypeStruct((ROWS, LANES), F32),
-            jax.ShapeDtypeStruct((ZO * ROWS, LANES), F32),
-            jax.ShapeDtypeStruct((ZO * ROWS, LANES), F32),
-        ],
+        out_shape=shapes,
         in_specs=[hbm] * 11,
         out_specs=[vmem] * 4,
         scratch_shapes=scratch,
@@ -781,6 +791,14 @@
         flat(ice_force), flat(ice_visc), held(ice_drag), held(ice_mask), held(ice_thick), held(ice_target),
         flat(ocean_temp), flat(ocean_salt), held(ocean_diff), held(ocean_mask), held(ocean_source),
     )
+    velocity, thickness, temp, salt = pl.pallas_call(
+        write_out,
+        out_shape=shapes,
+        in_specs=[pl.BlockSpec(memory_space=pl.ANY)] * 4,
+        out_specs=[pl.BlockSpec(memory_space=pl.ANY)] * 4,
+        scratch_shapes=[dma((4,))],
+        compiler_params=pltpu.CompilerParams(vmem_limit_bytes=1024 * 1024),
+    )(*results)
     return (
         velocity.reshape(ice_force.shape),
         thickness,

time: 51.8 us -> 49.2 us (0.950)
  local copies, waits for them, and re-layouts: 3.45 us -> 0 us
    unnamed x4 -> x0, local copies, waits for them, and re-layouts: 3.45 us -> none
    pallas_call x1 -> x2, Pallas kernels: 47.6 us -> 48 us  [the longest x1 46.4 us: per_device(): pl.pallas_call(kernel, out_shape=shapes, in_specs=[hbm] * 11, out_specs=[...]
where the time goes in v4:
time: 49.2 us; the launch traced here: 48.7 us
  Pallas kernels  48 us (98%)
  between operations  0.64 us (1%)
    pallas_call x1, Pallas kernels, per_device(): pl.pallas_call(kernel, out_shape=shapes, in_specs=[hbm] * 11, out_specs=[...  46.4 us
    pallas_call x1, Pallas kernels, per_device(): pl.pallas_call(write_out, out_shape=shapes, in_specs=[pl.BlockSpec(memory...  1.65 us

profile of v4, /device:TPU:0, one launch (start us, length us, event | category | flops | bytes accessed | tf_op | source)
XLA Modules:
  0.0 48.7 jit_solution(6880314684646223056)
XLA Ops:
  0.6 46.4 %shard_map.138 = (f32[704,128]{1,0:T(8,128)S(1)}, f32[32,128]{1,0:T(8,128)S(1)}, f32[2560,128]{1,0:T(8,128)S(1)}, f32[2560,128]{1,0:T(8,128)S(1)}) custom-call(f32[704,128]{1,0:T(8,128)} %bitcast.9, f32[320,128]{1,0:T(8,128)} %bitcast.10, f32[32,128]{1,0:T(8,128)} %drag_in.1, s32[32,128]{1,0:T(8,128)} %imask_in.1, f32[32,128]{1,0:T(8,128)} %thick_in.1, ...), custom_call_target="tpu_custom_call" | custom-call | tf_op jit(solution)/shard_map/pallas_call | solution.py:781
  47.0 1.6 %shard_map.139 = (f32[704,128]{1,0:T(8,128)}, f32[32,128]{1,0:T(8,128)}, f32[2560,128]{1,0:T(8,128)}, f32[2560,128]{1,0:T(8,128)}) custom-call(f32[704,128]{1,0:T(8,128)S(1)} %get-tuple-element.12.refs_0_, f32[32,128]{1,0:T(8,128)S(1)} %get-tuple-element.13.refs_1_, f32[2560,128]{1,0:T(8,128)S(1)} %get-tuple-element.14.refs_2_, ...), custom_call_target="tpu_custom_call" | custom-call | tf_op jit(solution)/shard_map/pallas_call | solution.py:794

commit v5 on v4

--- a/solution.py
+++ b/solution.py
@@ -310,12 +310,14 @@
             if "low" in ends:
                 ref[pl.ds(base + (ZO + 1) * ROWS, ROWS)] = ref[pl.ds(base + ZO * ROWS, ROWS)]
 
-    def put_pack(r, group, field, chunk, t, acc):
+    def put_pack(r, group, field, chunk, t, values):
         first, lane = packed_place(group, field, chunk)
         rows = pl.ds(first + t * SUB, SUB)
-        shifted = roll(acc, lane, 1)
-        mine = (lane8 >= lane) & (lane8 < lane + 16)
-        opack[r, rows] = jnp.where(mine, shifted, opack[r, rows])
+        pair = pair8 - lane // 2
+        acc = opack[r, rows]
+        for j, value in enumerate(values):
+            acc = jnp.where(pair == j, roll(value, lane + 2 * j + 1, 1), acc)
+        opack[r, rows] = acc
 
     def put_rows(r, ref, group, field, chunk):
         base = FBASE + field * FSPAN + ROWS + chunk * (CHUNK * ROWS)
@@ -330,11 +332,8 @@
             if not isinstance(base, int):
                 base = pl.multiple_of(base, SUB)
             for t in range(TILES):
-                acc = jnp.zeros((SUB, LANES), F32)
-                for j in range(CHUNK):
-                    value = fa[pl.ds(base + j * ROWS + t * SUB, SUB)]
-                    acc = jnp.where(pair8 == j, roll(value, 2 * j + 1, 1), acc)
-                put_pack(0, group, field, chunk, t, acc)
+                values = [fa[pl.ds(base + j * ROWS + t * SUB, SUB)] for j in range(CHUNK)]
+                put_pack(0, group, field, chunk, t, values)
             put_rows(0, fa, group, field, chunk)
 
     def over_chunks(group, step):
@@ -503,8 +502,6 @@
                     base = pl.multiple_of(base, SUB)
                 vec, lane = packed_place(group, field, chunk)
                 packed = merged[pl.ds(vec + t * SUB, SUB)]
-                packed = roll(packed, -lane if isinstance(lane, int) else lax.rem(LANES - lane, LANES), 1)
-                acc = jnp.zeros((SUB, LANES), F32)
                 prev = src[pl.ds(base - ROWS, SUB)]
                 cur = src[pl.ds(base, SUB)]
                 news = []
@@ -518,7 +515,7 @@
                         up = jnp.where(sub8 == 0, rrow[s, 0, pl.ds(level, 1)], up)
                     if t == TILES - 1:
                         down = jnp.where(sub8 == SUB - 1, rrow[s, 1, pl.ds(level, 1)], down)
-                    edge = roll(packed, 127 - 2 * j, 1)
+                    edge = roll(packed, 127 - 2 * j - lane, 1)
                     beside = pl.ds(field * CHUNK * ROWS + j * ROWS + t * SUB, SUB)
                     left = jnp.where(lane8 == 0, edge, sides[beside, :LANES])
                     right = jnp.where(lane8 == LANES - 1, edge, sides[beside, LANES:])
@@ -537,7 +534,6 @@
                 first[0][0] = temp_top - heat_factor * rate
                 first[1][0] = salt_top - salt_factor * rate * (salt_ref + salt_top) / salt_ref
             for field in range(2):
-                acc = jnp.zeros((SUB, LANES), F32)
                 for j in range(CHUNK):
                     new = first[field][j]
                     if s < STEPS - 1:
@@ -545,14 +541,13 @@
                         if not isinstance(row, int):
                             row = pl.multiple_of(row, SUB)
                         dst[pl.ds(row, SUB)] = new
-                        acc = jnp.where(pair8 == j, roll(new, 2 * j + 1, 1), acc)
                     else:
                         row = chunk * (CHUNK * ROWS) + j * ROWS + t * SUB
                         if not isinstance(row, int):
                             row = pl.multiple_of(row, SUB)
                         dst[field][pl.ds(row, SUB)] = new
                 if s < STEPS - 1:
-                    put_pack(s + 1, group, field, chunk, t, acc)
+                    put_pack(s + 1, group, field, chunk, t, first[field])
         if s < STEPS - 1:
             for field in range(2):
                 put_rows(s + 1, dst, group, field, chunk)

time: 49.2 us -> 48.2 us (0.980)
  Pallas kernels: 48 us -> 47.5 us
    pallas_call x1, Pallas kernels: 46.4 us -> 45.8 us  [per_device(): pl.pallas_call(kernel, out_shape=shapes, in_specs=[hbm] * 11, out_specs=[...]
where the time goes in v5:
time: 48.2 us; the launch traced here: 48.1 us
  Pallas kernels  47.5 us (99%)
  between operations  0.64 us (1%)
    pallas_call x1, Pallas kernels, per_device(): pl.pallas_call(kernel, out_shape=shapes, in_specs=[hbm] * 11, out_specs=[...  45.8 us
    pallas_call x1, Pallas kernels, per_device(): pl.pallas_call(write_out, out_shape=shapes, in_specs=[pl.BlockSpec(memory...  1.65 us

profile of v5, /device:TPU:0, one launch (start us, length us, event | category | flops | bytes accessed | tf_op | source)
XLA Modules:
  0.0 48.1 jit_solution(9274090897538664321)
XLA Ops:
  0.6 45.8 %shard_map.138 = (f32[704,128]{1,0:T(8,128)S(1)}, f32[32,128]{1,0:T(8,128)S(1)}, f32[2560,128]{1,0:T(8,128)S(1)}, f32[2560,128]{1,0:T(8,128)S(1)}) custom-call(f32[704,128]{1,0:T(8,128)} %bitcast.9, f32[320,128]{1,0:T(8,128)} %bitcast.10, f32[32,128]{1,0:T(8,128)} %drag_in.1, s32[32,128]{1,0:T(8,128)} %imask_in.1, f32[32,128]{1,0:T(8,128)} %thick_in.1, ...), custom_call_target="tpu_custom_call" | custom-call | tf_op jit(solution)/shard_map/pallas_call | solution.py:776
  46.4 1.6 %shard_map.139 = (f32[704,128]{1,0:T(8,128)}, f32[32,128]{1,0:T(8,128)}, f32[2560,128]{1,0:T(8,128)}, f32[2560,128]{1,0:T(8,128)}) custom-call(f32[704,128]{1,0:T(8,128)S(1)} %get-tuple-element.12.refs_0_, f32[32,128]{1,0:T(8,128)S(1)} %get-tuple-element.13.refs_1_, f32[2560,128]{1,0:T(8,128)S(1)} %get-tuple-element.14.refs_2_, ...), custom_call_target="tpu_custom_call" | custom-call | tf_op jit(solution)/shard_map/pallas_call | solution.py:789
